TPU v7x, 256 devices: a whole 4x4x8 slice. The times are simulated.
256 devices in a mesh: lon: 32 (over y_hi, z, core), lat: 8 (over x, y_lo).
Axes of the slice: x: 4, y: 4 (y_hi: 2, y_lo: 2; y = y_hi * 2 + y_lo), z: 8, core: 2. Of those that a mesh axis runs over, the one named last changes fastest.
Arguments:
- previous: float32 [2, 2, 1024, 8192], P(None, None, 'lon', 'lat'), may hold values from -6 to 6
- current: float32 [2, 2, 1024, 8192], P(None, None, 'lon', 'lat'), may hold values from -6 to 6
- east_speed: float32 [2, 1024, 8192], P(None, 'lon', 'lat'), may hold values from -0.28 to 0.28, as said below
- north_speed: float32 [2, 1024, 8192], P(None, 'lon', 'lat'), may hold values from -0.28 to 0.28, as said below
- east_mix: float32 [2, 1024, 8192], P(None, 'lon', 'lat'), may hold values from 0 to 0.1, as said below
- north_mix: float32 [2, 1024, 8192], P(None, 'lon', 'lat'), may hold values from 0 to 0.1, as said below
- sea_mask: int32 [1024, 8192], P('lon', 'lat'), may hold values from 0 to 1, as said below
Outputs:
- lagged: float32 [2, 2, 1024, 8192], P(None, None, 'lon', 'lat')
- latest: float32 [2, 2, 1024, 8192], P(None, None, 'lon', 'lat')
Inputs may be any that keep to these rules, and one draw needn't show every extreme that they name: `sea_mask`: the land cells form rectangular blocks of 32 x 1024 cells, coastal blocks with scattered land and open ocean with a few islands; which block is which is random. `east_speed`: zero on every face that touches a land cell; the east face of the last longitude joins it to the first. `north_speed`: zero on every face that touches a land cell and on the whole top latitude. `east_mix`: zero on every face that touches a land cell. `north_mix`: zero on every face that touches a land cell; on the top latitude the face across the fold joins cell i to cell 1024 - 1 - i and the value at i equals that at 1023 - i.
All inputs are finite; a program needn't handle non-finite values.
Results may differ from a plain program's by a relative error of at most 0.00002.
Values sent between devices are 32-bit elements; how exact they have to be, the bound alone decides.
A program may use at most 64 MiB of HBM per device.

v0:
```python
import functools

import jax
import jax.numpy as jnp
from jax import lax
from jax.experimental import pallas as pl
from jax.experimental.pallas import tpu as pltpu
from jax.sharding import PartitionSpec as P

STEPS = 6
GAMMA = 0.1
MESH = pl.DeviceIdType.MESH

LANES = 128
PAD = 16
HALO = 2 * STEPS
SLOT = 16
UNIT = HALO
ES, EM, NS, NM = 0, 2, 4, 6


def kernel(sizes, *refs):
    n_lon, n_lat, columns, height = sizes
    (prev_h, cur_h, es_h, ns_h, em_h, nm_h, mask_h, lag_h, lat_h) = refs[:9]
    (prev_v, cur_v, es_v, ns_v, em_v, nm_v, mask_v, state, coef, flux, pack, land) = refs[9:21]
    (in_sem, out_sem, lon_send, lon_recv, lat_send, lat_recv, self_sem) = refs[21:]
    tiles = height // LANES
    ring = tiles + 1
    row_tiles = columns // 8
    own = pl.ds(PAD, columns)

    lon, lat = lax.axis_index("lon"), lax.axis_index("lat")
    east, west = lax.rem(lon + 1, n_lon), lax.rem(lon + n_lon - 1, n_lon)
    is_top, is_bottom = lat == n_lat - 1, lat == 0
    north, south = jnp.minimum(lat + 1, n_lat - 1), jnp.maximum(lat - 1, 0)
    up_main = jnp.where(is_top, n_lon - 1 - lon, lon)
    up_east = jnp.where(is_top, lax.rem(n_lon - lon, n_lon), east)
    up_west = jnp.where(is_top, lax.rem(2 * n_lon - 2 - lon, n_lon), west)
    self_east = jnp.logical_and(is_top, up_east == lon)
    self_west = jnp.logical_and(is_top, up_west == lon)
    not_self_east = jnp.logical_not(self_east)
    not_self_west = jnp.logical_not(self_west)
    not_bottom = jnp.logical_not(is_bottom)

    staged = [
        (mask_h, mask_v), (cur_h, cur_v), (prev_h, prev_v),
        (es_h, es_v), (em_h, em_v), (ns_h, ns_v), (nm_h, nm_v),
    ]
    loads = [pltpu.make_async_copy(a, b, in_sem.at[i]) for i, (a, b) in enumerate(staged)]

    barrier = pltpu.get_barrier_semaphore()

    def greet(to_lon, to_lat):
        pl.semaphore_signal(
            barrier, inc=1, device_id={"lon": to_lon, "lat": to_lat}, device_id_type=MESH
        )

    greet(east, lat)
    greet(west, lat)
    greet(up_main, north)

    @pl.when(not_self_east)
    def _():
        greet(up_east, north)

    @pl.when(not_self_west)
    def _():
        greet(up_west, north)

    @pl.when(not_bottom)
    def _():
        greet(lon, south)
        greet(east, south)
        greet(west, south)

    for c in loads:
        c.start()

    for c in loads[:3]:
        c.wait()

    @pl.loop(0, tiles)
    def _(t):
        lanes = pl.ds(pl.multiple_of(t * LANES, LANES), LANES)
        for r in range(row_tiles):
            rows = slice(8 * r, 8 * r + 8)
            wet = mask_v[rows, lanes].astype(jnp.float32)
            for tr in range(2):
                for lv in range(2):
                    state[0, 1, tr, lv, t, PAD + 8 * r : PAD + 8 * r + 8, :] = (
                        cur_v[tr, lv, rows, lanes] * wet
                    )
                    state[0, 0, tr, lv, t, PAD + 8 * r : PAD + 8 * r + 8, :] = (
                        prev_v[tr, lv, rows, lanes] * wet
                    )

    for c in loads[3:]:
        c.wait()

    @pl.loop(0, tiles)
    def _(t):
        lanes = pl.ds(pl.multiple_of(t * LANES, LANES), LANES)
        for r in range(row_tiles):
            rows = slice(8 * r, 8 * r + 8)
            for field, ref, scale in (
                (ES, es_v, 2.0 / 12.0), (EM, em_v, 2.0), (NS, ns_v, 2.0 / 12.0), (NM, nm_v, 2.0),
            ):
                for lv in range(2):
                    coef[field + lv, t, PAD + 8 * r : PAD + 8 * r + 8, :] = (
                        ref[lv, rows, lanes] * scale
                    )

    lane = lax.broadcasted_iota(jnp.int32, (8, LANES), 1)
    sub = lax.broadcasted_iota(jnp.int32, (8, LANES), 0)
    slot_of_lane = lane // SLOT

    def field_rows(f, t, rows):
        if f < 8:
            return state[0, f // 4, (f // 2) % 2, f % 2, t, rows, :]
        return coef[f - 8, t, rows, :]

    top = jnp.where(is_top, 1, 0)
    turn = jnp.where(is_top, -1.0, 1.0)
    for r in range(row_tiles):
        rows = slice(PAD + 8 * r, PAD + 8 * r + 8)
        for h in range(2):
            up = jnp.zeros((8, LANES), jnp.float32)
            down = jnp.zeros((8, LANES), jnp.float32)
            for s in range(8):
                f = 8 * h + s
                here = slot_of_lane == s
                mine = field_rows(f, tiles - 1, rows)
                shift = (SLOT * s + SLOT) % LANES
                if f >= 8 + NS:
                    mine = pltpu.roll(mine, shift + top, 1)
                elif shift:
                    mine = pltpu.roll(mine, shift, 1)
                if f - 8 in (ES, ES + 1, NS, NS + 1):
                    mine = mine * turn
                up = jnp.where(here, mine, up)
                mine = field_rows(f, 0, rows)
                if s:
                    mine = pltpu.roll(mine, SLOT * s, 1)
                down = jnp.where(here, mine, down)
            pack[0, h, 8 * r : 8 * r + 8, :] = up
            pack[1, h, 8 * r : 8 * r + 8, :] = down

    @pl.when(is_top)
    def _():
        for h in range(2):
            turned = []
            for r in range(row_tiles):
                x = pack[0, h, 8 * r : 8 * r + 8, :]
                for bit in (1, 2, 4, 8):
                    x = jnp.where(
                        (lane & bit) == 0,
                        pltpu.roll(x, LANES - bit, 1),
                        pltpu.roll(x, bit, 1),
                    )
                for bit in (1, 2, 4):
                    x = jnp.where(
                        (sub & bit) == 0, pltpu.roll(x, 8 - bit, 0), pltpu.roll(x, bit, 0)
                    )
                turned.append(x)
            for r in range(row_tiles):
                pack[0, h, 8 * r : 8 * r + 8, :] = turned[row_tiles - 1 - r]

    @pl.when(is_bottom)
    def _():
        land[0] = jnp.zeros(land.shape[1:], jnp.float32)

    peers = 8 - jnp.where(is_bottom, 3, 0) - jnp.where(self_east, 1, 0) - jnp.where(self_west, 1, 0)
    pl.semaphore_wait(barrier, peers)

    own_rows = pl.ds(0, columns)
    last_rows, first_rows = pl.ds(columns - HALO, HALO), pl.ds(0, HALO)
    west_rows, east_rows = pl.ds(PAD - HALO, HALO), pl.ds(PAD + columns, HALO)

    def lat_copy(out, src_rows, side, dst_rows, slot, to_lon, to_lat):
        return pltpu.make_async_remote_copy(
            src_ref=pack.at[out, :, src_rows, :],
            dst_ref=land.at[side, :, dst_rows, :],
            send_sem=lat_send.at[out, slot],
            recv_sem=lat_recv.at[side, slot],
            device_id={"lon": to_lon, "lat": to_lat},
            device_id_type=MESH,
        )

    up_main_copy = lat_copy(0, own_rows, top, own, 0, up_main, north)
    up_east_copy = lat_copy(0, last_rows, top, west_rows, 1, up_east, north)
    up_west_copy = lat_copy(0, first_rows, top, east_rows, 2, up_west, north)
    down_copies = [
        lat_copy(1, own_rows, 1, own, 0, lon, south),
        lat_copy(1, last_rows, 1, west_rows, 1, east, south),
        lat_copy(1, first_rows, 1, east_rows, 2, west, south),
    ]
    self_east_copy = pltpu.make_async_copy(
        pack.at[0, :, last_rows, :], land.at[1, :, west_rows, :], self_sem.at[0]
    )
    self_west_copy = pltpu.make_async_copy(
        pack.at[0, :, first_rows, :], land.at[1, :, east_rows, :], self_sem.at[1]
    )

    up_main_copy.start()

    @pl.when(not_self_east)
    def _():
        up_east_copy.start()

    @pl.when(not_self_west)
    def _():
        up_west_copy.start()

    @pl.when(self_east)
    def _():
        self_east_copy.start()

    @pl.when(self_west)
    def _():
        self_west_copy.start()

    @pl.when(not_bottom)
    def _():
        for c in down_copies:
            c.start()

    def lon_copies(way, to_lon):
        newer, older, faces, cells = HALO, HALO - 1, HALO - 1, HALO - 2
        if way == 1:
            faces = cells

        def part(ref, width):
            if way == 0:
                src, dst = PAD + columns - width, PAD - width
            else:
                src, dst = PAD, PAD + columns
            return ref.at[..., pl.ds(src, width), :], ref.at[..., pl.ds(dst, width), :]

        parts = [
            part(state.at[0, 1, :, :, pl.ds(0, tiles)], newer),
            part(state.at[0, 0, :, :, pl.ds(0, tiles)], older),
            part(coef.at[pl.ds(ES, 4), pl.ds(0, tiles)], faces),
            part(coef.at[pl.ds(NS, 4), pl.ds(0, tiles)], cells),
        ]
        return [
            pltpu.make_async_remote_copy(
                src_ref=src,
                dst_ref=dst,
                send_sem=lon_send.at[way, i],
                recv_sem=lon_recv.at[way, i],
                device_id={"lon": to_lon, "lat": lat},
                device_id_type=MESH,
            )
            for i, (src, dst) in enumerate(parts)
        ]

    eastward, westward = lon_copies(0, east), lon_copies(1, west)
    for a, b in zip(eastward, westward):
        a.start()
        b.start()

    first_lane, last_lane = lane == 0, lane == LANES - 1

    def unit(k, r0, outs):
        wide = [(outs[0] - 1) % ring] + list(outs)
        beyond = (outs[-1] + 1) % ring

        @pl.loop(0, 2)
        def _(lv):
            for tr in range(2):
                older = state.at[k - 1, 0, tr, lv]
                newer = state.at[k - 1, 1, tr, lv]
                older_next = state.at[k, 0, tr, lv]
                newer_next = state.at[k, 1, tr, lv]
                es, em = coef.at[ES + lv], coef.at[EM + lv]
                ns, nm = coef.at[NS + lv], coef.at[NM + lv]

                def east_flux(t, r):
                    def q(ref, d):
                        return ref[t, pl.ds(r + d, 8), :]

                    near = q(newer, 0) + q(newer, 1)
                    far = q(newer, -1) + q(newer, 2)
                    return q(es, 0) * (7.0 * near - far) - q(em, 0) * (q(older, 1) - q(older, 0))

                low = {}
                high = {}
                for t in outs:
                    low[t] = east_flux(t, r0 - 1)
                    high[t] = east_flux(t, r0 + 4)
                    flux[t, 0:8, :] = low[t]
                    flux[t, 5:13, :] = high[t]

                for window in range(2):
                    r = r0 + 4 * window
                    rows = pl.ds(r, 8)

                    n, o, s = {}, {}, {}
                    for t in wide + [beyond]:
                        n[t] = newer[t, rows, :]
                    back = {t: pltpu.roll(n[t], LANES - 1, 1) for t in n}
                    for t in wide:
                        n1 = jnp.where(last_lane, back[(t + 1) % ring], back[t])
                        s[t] = n[t] + n1
                    s_end = n[beyond] + back[beyond]
                    s_back = {t: pltpu.roll(s[t], LANES - 1, 1) for t in wide}
                    s_back_end = pltpu.roll(s_end, LANES - 1, 1)
                    s_forth = {t: pltpu.roll(s[t], 1, 1) for t in wide}
                    for t in wide + [beyond]:
                        o[t] = older[t, rows, :]
                    o_back = {t: pltpu.roll(o[t], LANES - 1, 1) for t in o}
                    flow = {}
                    for i, t in enumerate(wide):
                        after = s_back[wide[i + 1]] if i + 1 < len(wide) else s_back_end
                        ahead = jnp.where(last_lane, after, s_back[t])
                        behind = s_forth[t]
                        if i > 0:
                            behind = jnp.where(first_lane, s_forth[wide[i - 1]], behind)
                        grad = jnp.where(last_lane, o_back[(t + 1) % ring], o_back[t]) - o[t]
                        flow[t] = (
                            ns[t, rows, :] * (8.0 * s[t] - (ahead + behind)) - nm[t, rows, :] * grad
                        )
                    flow_forth = {t: pltpu.roll(flow[t], 1, 1) for t in wide}
                    for i, t in enumerate(outs):
                        north_div = flow[t] - jnp.where(
                            first_lane, flow_forth[wide[i]], flow_forth[t]
                        )
                        if window == 0:
                            east_div = flux[t, 1:9, :] - low[t]
                        else:
                            east_div = high[t] - flux[t, 4:12, :]
                        fresh = o[t] - (east_div + north_div)
                        newer_next[t, rows, :] = fresh
                        older_next[t, rows, :] = (1.0 - 2.0 * GAMMA) * n[t] + GAMMA * (o[t] + fresh)

    def inner_place(u):
        k = jnp.where(u < 3, 1, jnp.where(u > 9, 6, (u - 3) // 2 + 2))
        j = jnp.where(u < 3, u, jnp.where(u < 9, lax.rem(u - 3, 2), 0))
        gap = jnp.where(u < 3, 8, 20 - 4 * k)
        return k, PAD + jnp.minimum(2 * k, 10) + j * gap

    @pl.loop(0, 11)
    def _(u):
        k, r0 = inner_place(u)
        unit(k, r0, list(range(tiles)))

    lat_in_south = [
        lat_copy(0, own_rows, 0, own, 0, lon, lat),
        lat_copy(0, last_rows, 0, west_rows, 1, lon, lat),
        lat_copy(0, first_rows, 0, east_rows, 2, lon, lat),
    ]

    @pl.when(not_bottom)
    def _():
        for c in lat_in_south:
            c.wait_recv()

    down_copies[0].wait_recv()

    @pl.when(not_self_east)
    def _():
        down_copies[1].wait_recv()

    @pl.when(not_self_west)
    def _():
        down_copies[2].wait_recv()

    @pl.when(self_east)
    def _():
        self_east_copy.wait()

    @pl.when(self_west)
    def _():
        self_west_copy.wait()

    for r in range((columns + 2 * PAD) // 8 - 1):
        begin = PAD - HALO + 8 * r
        rows = slice(begin, begin + 8)
        for f in range(16):
            h, s = divmod(f, 8)
            if f in (8 + ES, 9 + ES, 8 + EM, 9 + EM):
                north_part = land[1, h, pl.ds(begin + top, 8), :]
            else:
                north_part = land[1, h, rows, :]
            if s:
                north_part = pltpu.roll(north_part, LANES - SLOT * s, 1)
            south_part = land[0, h, rows, :]
            if s < 7:
                south_part = pltpu.roll(south_part, LANES - SLOT - SLOT * s, 1)
            both = jnp.where(lane < SLOT, north_part, south_part)
            if f < 8:
                state[0, f // 4, (f // 2) % 2, f % 2, tiles, rows, :] = both
            else:
                coef[f - 8, tiles, rows, :] = both

    @pl.loop(0, 11)
    def _(u):
        k, r0 = inner_place(u)
        unit(k, r0, [tiles - 1, tiles, 0])

    even = lax.rem(lon, 2) == 0

    def wait_west():
        for c in eastward:
            c.wait_recv()

    def wait_east():
        for c in westward:
            c.wait_recv()

    @pl.loop(0, 12)
    def _(u):
        late = u >= 6
        k = lax.rem(u, 6) + 1
        do_east = even != late

        @pl.when(jnp.logical_and(lax.rem(u, 6) == 0, do_east))
        def _():
            wait_east()

        @pl.when(jnp.logical_and(lax.rem(u, 6) == 0, jnp.logical_not(do_east)))
        def _():
            wait_west()

        r0 = jnp.where(do_east, PAD + columns - 2 * k, PAD + 2 * k - UNIT)
        unit(k, r0, list(range(ring)))

    stores = []
    for kind, ref in ((0, lag_h), (1, lat_h)):
        for t in range(tiles):
            c = pltpu.make_async_copy(
                state.at[STEPS, kind, :, :, t, own, :],
                ref.at[:, :, :, pl.ds(t * LANES, LANES)],
                out_sem.at[kind, t],
            )
            c.start()
            stores.append(c)

    for a, b in zip(eastward, westward):
        a.wait_send()
        b.wait_send()
    up_main_copy.wait_send()

    @pl.when(not_self_east)
    def _():
        up_east_copy.wait_send()

    @pl.when(not_self_west)
    def _():
        up_west_copy.wait_send()

    @pl.when(not_bottom)
    def _():
        for c in down_copies:
            c.wait_send()

    for c in stores:
        c.wait()


def solution(mesh):
    n_lon, n_lat = mesh.shape["lon"], mesh.shape["lat"]

    def shards(previous, current, east_speed, north_speed, east_mix, north_mix, sea_mask):
        columns, height = previous.shape[2:]
        tiles = height // LANES
        rows = columns + 2 * PAD
        field = jax.ShapeDtypeStruct(previous.shape, jnp.float32)
        f32 = jnp.float32
        return pl.pallas_call(
            functools.partial(kernel, (n_lon, n_lat, columns, height)),
            out_shape=(field, field),
            in_specs=[pl.BlockSpec(memory_space=pl.ANY)] * 7,
            out_specs=[pl.BlockSpec(memory_space=pl.ANY)] * 2,
            scratch_shapes=[
                pltpu.VMEM(previous.shape, f32),
                pltpu.VMEM(current.shape, f32),
                pltpu.VMEM(east_speed.shape, f32),
                pltpu.VMEM(north_speed.shape, f32),
                pltpu.VMEM(east_mix.shape, f32),
                pltpu.VMEM(north_mix.shape, f32),
                pltpu.VMEM(sea_mask.shape, sea_mask.dtype),
                pltpu.VMEM((STEPS + 1, 2, 2, 2, tiles + 1, rows, LANES), f32),
                pltpu.VMEM((8, tiles + 1, rows, LANES), f32),
                pltpu.VMEM((tiles + 1, 16, LANES), f32),
                pltpu.VMEM((2, 2, columns, LANES), f32),
                pltpu.VMEM((2, 2, rows, LANES), f32),
                pltpu.SemaphoreType.DMA((7,)),
                pltpu.SemaphoreType.DMA((2, tiles)),
                pltpu.SemaphoreType.DMA((2, 4)),
                pltpu.SemaphoreType.DMA((2, 4)),
                pltpu.SemaphoreType.DMA((2, 3)),
                pltpu.SemaphoreType.DMA((2, 3)),
                pltpu.SemaphoreType.DMA((2,)),
            ],
            compiler_params=pltpu.CompilerParams(
                collective_id=0, has_side_effects=True, vmem_limit_bytes=48 * 2**20
            ),
            cost_estimate=pl.CostEstimate(
                flops=30 * STEPS * previous.size, bytes_accessed=16 * previous.size, transcendentals=0
            ),
        )(previous, current, east_speed, north_speed, east_mix, north_mix, sea_mask)

    return jax.shard_map(
        shards,
        mesh=mesh,
        in_specs=(
            P(None, None, "lon", "lat"),
            P(None, None, "lon", "lat"),
            P(None, "lon", "lat"),
            P(None, "lon", "lat"),
            P(None, "lon", "lat"),
            P(None, "lon", "lat"),
            P("lon", "lat"),
        ),
        out_specs=(P(None, None, "lon", "lat"), P(None, None, "lon", "lat")),
        check_vma=False,
    )
```

profile of v0, /device:TPU:14, one launch (start us, length us, event | category | flops | bytes accessed | tf_op | source)
XLA Modules:
  0.0 72.7 jit_solution(14672807301937795813)
XLA Ops:
  0.6 0.0 copy-start
  0.6 1.0 %copy-done = f32[2,2,32,1024]{3,2,1,0:T(8,128)S(1)} copy-done((f32[2,2,32,1024]{3,2,1,0:T(8,128)S(1)}, f32[2,2,32,1024]{3,2,1,0:T(8,128)}, u32[]{:S(2)}) %copy-start) | copy-done | bytes 524312
  1.7 0.0 copy-start.1
  1.7 1.0 %copy-done.1 = f32[2,2,32,1024]{3,2,1,0:T(8,128)S(1)} copy-done((f32[2,2,32,1024]{3,2,1,0:T(8,128)S(1)}, f32[2,2,32,1024]{3,2,1,0:T(8,128)}, u32[]{:S(2)}) %copy-start.1) | copy-done | bytes 524312
  2.7 0.0 copy-start.2
  2.7 0.9 %copy-done.2 = f32[2,32,1024]{2,1,0:T(8,128)S(1)} copy-done((f32[2,32,1024]{2,1,0:T(8,128)S(1)}, f32[2,32,1024]{2,1,0:T(8,128)}, u32[]{:S(2)}) %copy-start.2) | copy-done | bytes 262168
  3.7 0.0 copy-start.3
  3.7 0.9 %copy-done.3 = f32[2,32,1024]{2,1,0:T(8,128)S(1)} copy-done((f32[2,32,1024]{2,1,0:T(8,128)S(1)}, f32[2,32,1024]{2,1,0:T(8,128)}, u32[]{:S(2)}) %copy-start.3) | copy-done | bytes 262168
  4.6 0.0 copy-start.4
  4.6 0.9 %copy-done.4 = f32[2,32,1024]{2,1,0:T(8,128)S(1)} copy-done((f32[2,32,1024]{2,1,0:T(8,128)S(1)}, f32[2,32,1024]{2,1,0:T(8,128)}, u32[]{:S(2)}) %copy-start.4) | copy-done | bytes 262168
  5.6 0.0 copy-start.5
  5.6 0.9 %copy-done.5 = f32[2,32,1024]{2,1,0:T(8,128)S(1)} copy-done((f32[2,32,1024]{2,1,0:T(8,128)S(1)}, f32[2,32,1024]{2,1,0:T(8,128)}, u32[]{:S(2)}) %copy-start.5) | copy-done | bytes 262168
  6.5 0.0 copy-start.6
  6.5 0.9 %copy-done.6 = s32[32,1024]{1,0:T(8,128)S(1)} copy-done((s32[32,1024]{1,0:T(8,128)S(1)}, s32[32,1024]{1,0:T(8,128)}, u32[]{:S(2)}) %copy-start.6) | copy-done | bytes 131096
  7.4 63.7 %shard_map.86 = (f32[2,2,32,1024]{3,2,1,0:T(8,128)S(1)}, f32[2,2,32,1024]{3,2,1,0:T(8,128)S(1)}) custom-call(f32[2,2,32,1024]{3,2,1,0:T(8,128)S(1)} %copy-done, f32[2,2,32,1024]{3,2,1,0:T(8,128)S(1)} %copy-done.1, f32[2,32,1024]{2,1,0:T(8,128)S(1)} %copy-done.2, f32[2,32,1024]{2,1,0:T(8,128)S(1)} %copy-done.3, f32[2,32,1024]{2,1,0:T(8,128)S(1)} %copy-done.4, ...), custom_call_target="tpu_custom_call" | custom-call | flops 23592960 | bytes 2097152 | tf_op jit(solution)/shard_map/pallas_call | solution.py:470
  71.2 0.8 %copy.11 = f32[2,2,32,1024]{3,2,1,0:T(8,128)} copy(f32[2,2,32,1024]{3,2,1,0:T(8,128)S(1)} %get-tuple-element.4) | data formatting | bytes 1048576
  72.0 0.8 %copy.12 = f32[2,2,32,1024]{3,2,1,0:T(8,128)} copy(f32[2,2,32,1024]{3,2,1,0:T(8,128)S(1)} %get-tuple-element.5) | data formatting | bytes 1048576
Async XLA Ops:
  0.6 1.0 %copy-start = (f32[2,2,32,1024]{3,2,1,0:T(8,128)S(1)}, f32[2,2,32,1024]{3,2,1,0:T(8,128)}, u32[]{:S(2)}) copy-start(f32[2,2,32,1024]{3,2,1,0:T(8,128)} %refs_0_.1) | copy-start | bytes 1572868
  1.7 1.0 %copy-start.1 = (f32[2,2,32,1024]{3,2,1,0:T(8,128)S(1)}, f32[2,2,32,1024]{3,2,1,0:T(8,128)}, u32[]{:S(2)}) copy-start(f32[2,2,32,1024]{3,2,1,0:T(8,128)} %refs_1_.1) | copy-start | bytes 1572868
  2.7 0.9 %copy-start.2 = (f32[2,32,1024]{2,1,0:T(8,128)S(1)}, f32[2,32,1024]{2,1,0:T(8,128)}, u32[]{:S(2)}) copy-start(f32[2,32,1024]{2,1,0:T(8,128)} %refs_2_.1) | copy-start | bytes 786436
  3.7 0.9 %copy-start.3 = (f32[2,32,1024]{2,1,0:T(8,128)S(1)}, f32[2,32,1024]{2,1,0:T(8,128)}, u32[]{:S(2)}) copy-start(f32[2,32,1024]{2,1,0:T(8,128)} %refs_3_.1) | copy-start | bytes 786436
  4.6 0.9 %copy-start.4 = (f32[2,32,1024]{2,1,0:T(8,128)S(1)}, f32[2,32,1024]{2,1,0:T(8,128)}, u32[]{:S(2)}) copy-start(f32[2,32,1024]{2,1,0:T(8,128)} %refs_4_.1) | copy-start | bytes 786436
  5.6 0.9 %copy-start.5 = (f32[2,32,1024]{2,1,0:T(8,128)S(1)}, f32[2,32,1024]{2,1,0:T(8,128)}, u32[]{:S(2)}) copy-start(f32[2,32,1024]{2,1,0:T(8,128)} %refs_5_.1) | copy-start | bytes 786436
  6.5 0.9 %copy-start.6 = (s32[32,1024]{1,0:T(8,128)S(1)}, s32[32,1024]{1,0:T(8,128)}, u32[]{:S(2)}) copy-start(s32[32,1024]{1,0:T(8,128)} %refs_6_.1) | copy-start | bytes 393220
where the time goes:
time: 73.4 us; the launch traced here: 72.7 us
  Pallas kernels  63.7 us (87%)
  local copies, waits for them, and re-layouts  8.37 us (11%)
    pallas_call x1, Pallas kernels, shards(): pl.pallas_call(functools.partial(kernel, (n_lon, n_lat, columns, height))...  63.7 us
    unnamed x16, local copies, waits for them, and re-layouts  8.37 us

commit v1 on v0

v1 whole, which is shorter than its diff:
```python
import functools

import jax
import jax.numpy as jnp
from jax import lax
from jax.experimental import pallas as pl
from jax.experimental.pallas import tpu as pltpu
from jax.sharding import PartitionSpec as P

STEPS = 6
GAMMA = 0.1
MESH = pl.DeviceIdType.MESH

LANES = 128
PAD = 16
HALO = 2 * STEPS
SLOT = 16
UNIT = HALO
ES, EM, NS, NM = 0, 2, 4, 6


def kernel(sizes, *refs):
    n_lon, n_lat, columns, height = sizes
    (prev_h, cur_h, es_h, ns_h, em_h, nm_h, mask_h, lag_h, lat_h) = refs[:9]
    (prev_v, cur_v, es_v, ns_v, em_v, nm_v, mask_v, state, coef, end_state, end_coef, flux, held, pack, land) = refs[9:24]
    (in_sem, out_sem, lon_send, lon_recv, lat_send, lat_recv, self_sem) = refs[24:]
    tiles = height // LANES
    ring = tiles + 1
    row_tiles = columns // 8
    own = pl.ds(PAD, columns)

    lon, lat = lax.axis_index("lon"), lax.axis_index("lat")
    east, west = lax.rem(lon + 1, n_lon), lax.rem(lon + n_lon - 1, n_lon)
    is_top, is_bottom = lat == n_lat - 1, lat == 0
    top = jnp.where(is_top, 1, 0)
    north, south = jnp.minimum(lat + 1, n_lat - 1), jnp.maximum(lat - 1, 0)
    up_main = jnp.where(is_top, n_lon - 1 - lon, lon)
    up_east = jnp.where(is_top, lax.rem(n_lon - lon, n_lon), east)
    up_west = jnp.where(is_top, lax.rem(2 * n_lon - 2 - lon, n_lon), west)
    self_east = jnp.logical_and(is_top, up_east == lon)
    self_west = jnp.logical_and(is_top, up_west == lon)
    not_self_east = jnp.logical_not(self_east)
    not_self_west = jnp.logical_not(self_west)
    not_bottom = jnp.logical_not(is_bottom)

    staged = [
        (mask_h, mask_v), (cur_h, cur_v), (prev_h, prev_v),
        (es_h, es_v), (em_h, em_v), (ns_h, ns_v), (nm_h, nm_v),
    ]
    loads = [pltpu.make_async_copy(a, b, in_sem.at[i]) for i, (a, b) in enumerate(staged)]

    barrier = pltpu.get_barrier_semaphore()

    def greet(to_lon, to_lat):
        pl.semaphore_signal(
            barrier, inc=1, device_id={"lon": to_lon, "lat": to_lat}, device_id_type=MESH
        )

    greet(east, lat)
    greet(west, lat)
    greet(up_main, north)

    @pl.when(not_self_east)
    def _():
        greet(up_east, north)

    @pl.when(not_self_west)
    def _():
        greet(up_west, north)

    @pl.when(not_bottom)
    def _():
        greet(lon, south)
        greet(east, south)
        greet(west, south)

    for c in loads:
        c.start()

    lane = lax.broadcasted_iota(jnp.int32, (8, LANES), 1)
    sub = lax.broadcasted_iota(jnp.int32, (8, LANES), 0)

    def roll(x, shift):
        return pltpu.roll(x, shift % LANES, 1)

    def exchange(tile):
        for bit in (1, 2, 4):
            keep = (lane & bit) == 0
            new = list(tile)
            for t in range(tiles):
                if not t & bit:
                    x, y = tile[t], tile[t + bit]
                    new[t] = jnp.where(keep, x, roll(y, bit))
                    new[t + bit] = jnp.where(keep, roll(x, -bit), y)
            tile = new
        return tile

    def lay_out(pieces):
        for load, target, ends, r in pieces:
            tile = [load(slice(8 * r, 8 * r + 8), slice(t * LANES, (t + 1) * LANES)) for t in range(tiles)]
            rows = slice(PAD + 8 * r, PAD + 8 * r + 8)
            both = jnp.where(lane < LANES // 2, roll(tile[0], HALO), roll(tile[-1], -HALO))
            target[tiles, rows, :] = both
            ends[8 * r : 8 * r + 8, :] = both
            for t, x in enumerate(exchange(tile)):
                target[t, rows, :] = x

    def masked(ref, tr, lv):
        return lambda rows, lanes: ref[tr, lv, rows, lanes] * mask_v[rows, lanes].astype(jnp.float32)

    def scaled(ref, lv, scale):
        return lambda rows, lanes: ref[lv, rows, lanes] * scale

    def level(kind, ref):
        lay_out([
            (masked(ref, tr, lv), state.at[0, kind, tr, lv], end_state.at[kind, tr, lv], r)
            for tr in range(2) for lv in range(2) for r in range(row_tiles)
        ])

    def coefs(*fields):
        lay_out([
            (scaled(ref, lv, scale), coef.at[field + lv], end_coef.at[field + lv], r)
            for field, ref, scale in fields for lv in range(2) for r in range(row_tiles)
        ])

    loads[0].wait()
    loads[1].wait()
    level(1, cur_v)
    loads[2].wait()
    level(0, prev_v)

    def lon_copies(way, to_lon):
        newer, older, faces, cells = HALO, HALO - 1, HALO - 1, HALO - 2
        if way == 1:
            faces = cells

        def part(ref, ends, width):
            begin = columns - width if way == 0 else 0
            dst = pl.ds(PAD - width if way == 0 else PAD + columns, width)
            return [
                (ref.at[..., pl.ds(0, tiles), pl.ds(PAD + begin, width), :], ref.at[..., pl.ds(0, tiles), dst, :]),
                (ends.at[..., pl.ds(begin, width), :], ref.at[..., tiles, dst, :]),
            ]

        parts = (
            part(state.at[0, 1], end_state.at[1], newer)
            + part(state.at[0, 0], end_state.at[0], older)
            + part(coef.at[pl.ds(ES, 4)], end_coef.at[pl.ds(ES, 4)], faces)
            + part(coef.at[pl.ds(NS, 4)], end_coef.at[pl.ds(NS, 4)], cells)
        )
        return [
            pltpu.make_async_remote_copy(
                src_ref=src,
                dst_ref=dst,
                send_sem=lon_send.at[way, i],
                recv_sem=lon_recv.at[way, i],
                device_id={"lon": to_lon, "lat": lat},
                device_id_type=MESH,
            )
            for i, (src, dst) in enumerate(parts)
        ]

    eastward, westward = lon_copies(0, east), lon_copies(1, west)
    peers = 8 - jnp.where(is_bottom, 3, 0) - jnp.where(self_east, 1, 0) - jnp.where(self_west, 1, 0)
    pl.semaphore_wait(barrier, peers)

    def send(first, last):
        for i in range(first, last):
            eastward[i].start()
            westward[i].start()

    send(0, 4)
    loads[3].wait()
    loads[4].wait()
    coefs((ES, es_v, 2.0 / 12.0), (EM, em_v, 2.0))
    send(4, 6)
    loads[5].wait()
    loads[6].wait()
    coefs((NS, ns_v, 2.0 / 12.0), (NM, nm_v, 2.0))
    send(6, 8)

    slot_of_lane = lane // SLOT

    def field_rows(f, rows):
        if f < 8:
            return end_state[f // 4, (f // 2) % 2, f % 2, rows, :]
        return end_coef[f - 8, rows, :]

    turn = jnp.where(is_top, -1.0, 1.0)
    for r in range(row_tiles):
        rows = slice(8 * r, 8 * r + 8)
        for h in range(2):
            up = jnp.zeros((8, LANES), jnp.float32)
            down = jnp.zeros((8, LANES), jnp.float32)
            for s in range(8):
                f = 8 * h + s
                here = slot_of_lane == s
                mine = field_rows(f, rows)
                shift = (SLOT * s - (LANES - HALO - SLOT)) % LANES
                if f >= 8 + NS:
                    high = pltpu.roll(mine, shift + top, 1)
                else:
                    high = roll(mine, shift)
                if f - 8 in (ES, ES + 1, NS, NS + 1):
                    high = high * turn
                up = jnp.where(here, high, up)
                down = jnp.where(here, roll(mine, SLOT * s - HALO), down)
            pack[0, h, 8 * r : 8 * r + 8, :] = up
            pack[1, h, 8 * r : 8 * r + 8, :] = down

    @pl.when(is_top)
    def _():
        for h in range(2):
            turned = []
            for r in range(row_tiles):
                x = pack[0, h, 8 * r : 8 * r + 8, :]
                for bit in (1, 2, 4, 8):
                    x = jnp.where(
                        (lane & bit) == 0,
                        pltpu.roll(x, LANES - bit, 1),
                        pltpu.roll(x, bit, 1),
                    )
                for bit in (1, 2, 4):
                    x = jnp.where(
                        (sub & bit) == 0, pltpu.roll(x, 8 - bit, 0), pltpu.roll(x, bit, 0)
                    )
                turned.append(x)
            for r in range(row_tiles):
                pack[0, h, 8 * r : 8 * r + 8, :] = turned[row_tiles - 1 - r]

    @pl.when(is_bottom)
    def _():
        land[0] = jnp.zeros(land.shape[1:], jnp.float32)

    own_rows = pl.ds(0, columns)
    last_rows, first_rows = pl.ds(columns - HALO, HALO), pl.ds(0, HALO)
    west_rows, east_rows = pl.ds(PAD - HALO, HALO), pl.ds(PAD + columns, HALO)

    def lat_copy(out, src_rows, side, dst_rows, slot, to_lon, to_lat):
        return pltpu.make_async_remote_copy(
            src_ref=pack.at[out, :, src_rows, :],
            dst_ref=land.at[side, :, dst_rows, :],
            send_sem=lat_send.at[out, slot],
            recv_sem=lat_recv.at[side, slot],
            device_id={"lon": to_lon, "lat": to_lat},
            device_id_type=MESH,
        )

    up_main_copy = lat_copy(0, own_rows, top, own, 0, up_main, north)
    up_east_copy = lat_copy(0, last_rows, top, west_rows, 1, up_east, north)
    up_west_copy = lat_copy(0, first_rows, top, east_rows, 2, up_west, north)
    down_copies = [
        lat_copy(1, own_rows, 1, own, 0, lon, south),
        lat_copy(1, last_rows, 1, west_rows, 1, east, south),
        lat_copy(1, first_rows, 1, east_rows, 2, west, south),
    ]
    self_east_copy = pltpu.make_async_copy(
        pack.at[0, :, last_rows, :], land.at[1, :, west_rows, :], self_sem.at[0]
    )
    self_west_copy = pltpu.make_async_copy(
        pack.at[0, :, first_rows, :], land.at[1, :, east_rows, :], self_sem.at[1]
    )

    up_main_copy.start()

    @pl.when(not_self_east)
    def _():
        up_east_copy.start()

    @pl.when(not_self_west)
    def _():
        up_west_copy.start()

    @pl.when(self_east)
    def _():
        self_east_copy.start()

    @pl.when(self_west)
    def _():
        self_west_copy.start()

    @pl.when(not_bottom)
    def _():
        for c in down_copies:
            c.start()

    def up(x):
        return jnp.where(lane >= LANES - 8, roll(x, -9), roll(x, -8))

    def down(x):
        return jnp.where(lane < 8, roll(x, 9), roll(x, 8))

    def after(x):
        return [roll(x[0], -1)] if len(x) == 1 else x[1:] + [up(x[0])]

    def before(x):
        return [roll(x[0], 1)] if len(x) == 1 else [down(x[-1])] + x[:-1]

    def advance(old, lv, r0, group):
        for t in group:
            es = [coef[ES + lv, t, pl.ds(r0 + d, 8), :] for d in (-1, 4)]
            em = [coef[EM + lv, t, pl.ds(r0 + d, 8), :] for d in (-1, 4)]
            for tr in range(2):
                for i, d in enumerate((-1, 4)):

                    def q(kind, by):
                        return old[kind, tr, lv, t, pl.ds(r0 + d + by, 8), :]

                    near, far = q(1, 0) + q(1, 1), q(1, -1) + q(1, 2)
                    flux[lv, tr, t, 5 * i : 5 * i + 8, :] = es[i] * (7.0 * near - far) - em[i] * (
                        q(0, 1) - q(0, 0)
                    )
        for w in range(2):
            rows = pl.ds(r0 + 4 * w, 8)
            ns = [coef[NS + lv, t, rows, :] for t in group]
            nm = [coef[NM + lv, t, rows, :] for t in group]
            for tr in range(2):
                n = [old[1, tr, lv, t, rows, :] for t in group]
                o = [old[0, tr, lv, t, rows, :] for t in group]
                s = [a + b for a, b in zip(n, after(n))]
                flow = [
                    u * (8.0 * here - (a + b)) - v * (o1 - o0)
                    for u, v, here, a, b, o1, o0 in zip(ns, nm, s, after(s), before(s), after(o), o)
                ]
                for i, (t, f, f0) in enumerate(zip(group, flow, before(flow))):
                    east_div = (
                        flux[lv, tr, t, 4 * w + 1 : 4 * w + 9, :] - flux[lv, tr, t, 4 * w : 4 * w + 8, :]
                    )
                    fresh = o[i] - (east_div + (f - f0))
                    held[lv, 1, tr, w, t] = fresh
                    held[lv, 0, tr, w, t] = (1.0 - 2.0 * GAMMA) * n[i] + GAMMA * (o[i] + fresh)

    def unit(k, r0, groups):
        old, new = state.at[k - 1], state.at[k]
        for lv in range(2):
            for group in groups:
                advance(old, lv, r0, group)
        for lv in range(2):
            for w in range(2):
                for tr in range(2):
                    for t in sum(groups, []):
                        for kind in range(2):
                            new[kind, tr, lv, t, pl.ds(r0 + 4 * w, 8), :] = held[lv, kind, tr, w, t]

    main, edge = list(range(tiles)), [tiles]

    def inner_place(u):
        k = jnp.where(u < 3, 1, jnp.where(u > 9, 6, (u - 3) // 2 + 2))
        j = jnp.where(u < 3, u, jnp.where(u < 9, lax.rem(u - 3, 2), 0))
        gap = jnp.where(u < 3, 8, 20 - 4 * k)
        return k, PAD + jnp.minimum(2 * k, 10) + j * gap

    @pl.loop(0, 11)
    def _(u):
        k, r0 = inner_place(u)
        unit(k, r0, [main])

    lat_in_south = [
        lat_copy(0, own_rows, 0, own, 0, lon, lat),
        lat_copy(0, last_rows, 0, west_rows, 1, lon, lat),
        lat_copy(0, first_rows, 0, east_rows, 2, lon, lat),
    ]

    @pl.when(not_bottom)
    def _():
        for c in lat_in_south:
            c.wait_recv()

    down_copies[0].wait_recv()

    @pl.when(not_self_east)
    def _():
        down_copies[1].wait_recv()

    @pl.when(not_self_west)
    def _():
        down_copies[2].wait_recv()

    @pl.when(self_east)
    def _():
        self_east_copy.wait()

    @pl.when(self_west)
    def _():
        self_west_copy.wait()

    def unpack(begins):
        done = []
        for begin in begins:
            rows = pl.ds(begin, 8)
            for f in range(16):
                h, s = divmod(f, 8)
                source = rows
                if f in (8 + ES, 9 + ES, 8 + EM, 9 + EM):
                    source = pl.ds(begin + top, 8)
                north_part = roll(land[1, h, source, :], LANES - HALO - SLOT * s)
                south_part = roll(land[0, h, rows, :], HALO - SLOT - SLOT * s)
                if f < 8:
                    target = state.at[0, f // 4, (f // 2) % 2, f % 2, tiles]
                else:
                    target = coef.at[f - 8, tiles]
                inside = jnp.where(lane < HALO, south_part, target[rows, :])
                done.append((target, rows, jnp.where(lane >= LANES - HALO, north_part, inside)))
        for target, rows, value in done:
            target[rows, :] = value

    unpack([PAD + 8 * r for r in range(row_tiles)])

    @pl.loop(0, 11)
    def _(u):
        k, r0 = inner_place(u)
        unit(k, r0, [edge])

    even = lax.rem(lon, 2) == 0

    def finish(first_row, slot):
        for r in range(2):
            rows = pl.ds(pl.multiple_of(first_row + 8 * r, 8), 8)
            source = pl.ds(pl.multiple_of(PAD + first_row + 8 * r, 8), 8)
            for kind, target in ((0, prev_v), (1, cur_v)):
                for tr in range(2):
                    for lv in range(2):
                        tile = exchange([state[STEPS, kind, tr, lv, t, source, :] for t in main])
                        ends = state[STEPS, kind, tr, lv, tiles, source, :]
                        tile[0] = jnp.where(lane < HALO, roll(ends, -HALO), tile[0])
                        tile[-1] = jnp.where(lane >= LANES - HALO, roll(ends, HALO), tile[-1])
                        for t in main:
                            target[tr, lv, rows, t * LANES : (t + 1) * LANES] = tile[t]
        rows = pl.ds(pl.multiple_of(first_row, 16), 16)
        copies = [
            pltpu.make_async_copy(
                source.at[:, :, rows, :], target.at[:, :, rows, :], out_sem.at[slot, i]
            )
            for i, (source, target) in enumerate(((prev_v, lag_h), (cur_v, lat_h)))
        ]
        for c in copies:
            c.start()
        return copies

    @pl.loop(0, 2)
    def _(late):
        do_east = even != (late == 1)

        @pl.when(do_east)
        def _():
            for c in westward:
                c.wait_recv()

        @pl.when(jnp.logical_not(do_east))
        def _():
            for c in eastward:
                c.wait_recv()

        side = jnp.where(do_east, PAD + columns, PAD - HALO)
        unpack([side, side + 4])

        @pl.loop(1, STEPS + 1)
        def _(k):
            unit(k, jnp.where(do_east, PAD + columns - 2 * k, PAD + 2 * k - UNIT), [main, edge])

        finish(jnp.where(do_east, columns // 2, 0), late)

    finished = [
        pltpu.make_async_copy(
            source.at[:, :, pl.ds(0, 16), :], target.at[:, :, pl.ds(0, 16), :], out_sem.at[slot, i]
        )
        for slot in range(2)
        for i, (source, target) in enumerate(((prev_v, lag_h), (cur_v, lat_h)))
    ]

    for a, b in zip(eastward, westward):
        a.wait_send()
        b.wait_send()
    up_main_copy.wait_send()

    @pl.when(not_self_east)
    def _():
        up_east_copy.wait_send()

    @pl.when(not_self_west)
    def _():
        up_west_copy.wait_send()

    @pl.when(not_bottom)
    def _():
        for c in down_copies:
            c.wait_send()

    for c in finished:
        c.wait()


def solution(mesh):
    n_lon, n_lat = mesh.shape["lon"], mesh.shape["lat"]

    def shards(previous, current, east_speed, north_speed, east_mix, north_mix, sea_mask):
        columns, height = previous.shape[2:]
        tiles = height // LANES
        rows = columns + 2 * PAD
        field = jax.ShapeDtypeStruct(previous.shape, jnp.float32)
        f32 = jnp.float32
        return pl.pallas_call(
            functools.partial(kernel, (n_lon, n_lat, columns, height)),
            out_shape=(field, field),
            in_specs=[pl.BlockSpec(memory_space=pl.ANY)] * 7,
            out_specs=[pl.BlockSpec(memory_space=pl.ANY)] * 2,
            scratch_shapes=[
                pltpu.VMEM(previous.shape, f32),
                pltpu.VMEM(current.shape, f32),
                pltpu.VMEM(east_speed.shape, f32),
                pltpu.VMEM(north_speed.shape, f32),
                pltpu.VMEM(east_mix.shape, f32),
                pltpu.VMEM(north_mix.shape, f32),
                pltpu.VMEM(sea_mask.shape, sea_mask.dtype),
                pltpu.VMEM((STEPS + 1, 2, 2, 2, tiles + 1, rows, LANES), f32),
                pltpu.VMEM((8, tiles + 1, rows, LANES), f32),
                pltpu.VMEM((2, 2, 2, columns, LANES), f32),
                pltpu.VMEM((8, columns, LANES), f32),
                pltpu.VMEM((2, 2, tiles + 1, 16, LANES), f32),
                pltpu.VMEM((2, 2, 2, 2, tiles + 1, 8, LANES), f32),
                pltpu.VMEM((2, 2, columns, LANES), f32),
                pltpu.VMEM((2, 2, rows, LANES), f32),
                pltpu.SemaphoreType.DMA((7,)),
                pltpu.SemaphoreType.DMA((2, 2)),
                pltpu.SemaphoreType.DMA((2, 8)),
                pltpu.SemaphoreType.DMA((2, 8)),
                pltpu.SemaphoreType.DMA((2, 3)),
                pltpu.SemaphoreType.DMA((2, 3)),
                pltpu.SemaphoreType.DMA((2,)),
            ],
            compiler_params=pltpu.CompilerParams(
                collective_id=0, has_side_effects=True, vmem_limit_bytes=60 * 2**20
            ),
            cost_estimate=pl.CostEstimate(
                flops=30 * STEPS * previous.size, bytes_accessed=16 * previous.size, transcendentals=0
            ),
        )(previous, current, east_speed, north_speed, east_mix, north_mix, sea_mask)

    return jax.shard_map(
        shards,
        mesh=mesh,
        in_specs=(
            P(None, None, "lon", "lat"),
            P(None, None, "lon", "lat"),
            P(None, "lon", "lat"),
            P(None, "lon", "lat"),
            P(None, "lon", "lat"),
            P(None, "lon", "lat"),
            P("lon", "lat"),
        ),
        out_specs=(P(None, None, "lon", "lat"), P(None, None, "lon", "lat")),
        check_vma=False,
    )
```

time: 73.4 us -> 43 us (0.59)
  the two profiles are of different devices: /device:TPU:14 before, /device:TPU:6 now
where the time goes in v1:
time: 43 us; the launch traced here: 42.8 us
  Pallas kernels  39.5 us (92%)
  local copies, waits for them, and re-layouts  2.74 us (6%)
  between operations  0.65 us (2%)
    pallas_call x1, Pallas kernels, shards(): pl.pallas_call(functools.partial(kernel, (n_lon, n_lat, columns, height))...  39.5 us
    unnamed x4, local copies, waits for them, and re-layouts  2.74 us

profile of v1, /device:TPU:6, one launch (start us, length us, event | category | flops | bytes accessed | tf_op | source)
XLA Modules:
  0.0 42.8 jit_solution(1282666541078373957)
XLA Ops:
  0.6 39.5 %shard_map.86 = (f32[2,2,32,1024]{3,2,1,0:T(8,128)}, f32[2,2,32,1024]{3,2,1,0:T(8,128)}) custom-call(f32[2,2,32,1024]{3,2,1,0:T(8,128)} %refs_0_.1, f32[2,2,32,1024]{3,2,1,0:T(8,128)} %refs_1_.1, f32[2,32,1024]{2,1,0:T(8,128)} %refs_2_.1, f32[2,32,1024]{2,1,0:T(8,128)} %refs_3_.1, f32[2,32,1024]{2,1,0:T(8,128)} %refs_4_.1, f32[2,32,1024]{2,1,0:T(8,128)} %refs_5_.1, ...), custom_call_target="tpu_custom_call" | custom-call | flops 23592960 | bytes 2097152 | tf_op jit(solution)/shard_map/pallas_call | solution.py:502
  40.1 0.0 copy-start
  40.1 1.9 %copy.11 = f32[2,2,32,1024]{3,2,1,0:T(8,128)} copy(f32[2,2,32,1024]{3,2,1,0:T(8,128)} %get-tuple-element.4) | data formatting | bytes 1048576
  42.0 0.0 copy-done
  42.0 0.8 %copy.12 = f32[2,2,32,1024]{3,2,1,0:T(8,128)} copy(f32[2,2,32,1024]{3,2,1,0:T(8,128)S(1)} %copy-done) | data formatting | bytes 1048576
Async XLA Ops:
  40.1 2.0 %copy-start = (f32[2,2,32,1024]{3,2,1,0:T(8,128)S(1)}, f32[2,2,32,1024]{3,2,1,0:T(8,128)}, u32[]{:S(2)}) copy-start(f32[2,2,32,1024]{3,2,1,0:T(8,128)} %get-tuple-element.5) | copy-start | bytes 1572868

commit v2 on v1

v2 whole, which is shorter than its diff:
```python
import functools

import jax
import jax.numpy as jnp
from jax import lax
from jax.experimental import pallas as pl
from jax.experimental.pallas import tpu as pltpu
from jax.sharding import PartitionSpec as P

STEPS = 6
GAMMA = 0.1
MESH = pl.DeviceIdType.MESH

LANES = 128
PAD = 16
HALO = 2 * STEPS
SLOT = 16
UNIT = HALO
OLD, NEW = 0, 1
ES, EM, NS, NM = range(4)
SCALES = (2.0 / 12.0, 2.0, 2.0 / 12.0, 2.0)


def kernel(sizes, *refs):
    n_lon, n_lat, columns, height = sizes
    (prev_h, cur_h, es_h, ns_h, em_h, nm_h, mask_h, lag_h, lat_h) = refs[:9]
    (mask_v, state_v, coef_v, state, coef, ends, div, held, pack, land) = refs[9:19]
    (in_sem, out_sem, lon_send, lon_recv, lat_send, lat_recv, self_sem) = refs[19:]
    tiles = height // LANES
    ring = tiles + 1
    row_tiles = columns // 8
    own = pl.ds(PAD, columns)

    lon, lat = lax.axis_index("lon"), lax.axis_index("lat")
    east, west = lax.rem(lon + 1, n_lon), lax.rem(lon + n_lon - 1, n_lon)
    is_top, is_bottom = lat == n_lat - 1, lat == 0
    top = jnp.where(is_top, 1, 0)
    north, south = jnp.minimum(lat + 1, n_lat - 1), jnp.maximum(lat - 1, 0)
    up_main = jnp.where(is_top, n_lon - 1 - lon, lon)
    up_east = jnp.where(is_top, lax.rem(n_lon - lon, n_lon), east)
    up_west = jnp.where(is_top, lax.rem(2 * n_lon - 2 - lon, n_lon), west)
    self_east = jnp.logical_and(is_top, up_east == lon)
    self_west = jnp.logical_and(is_top, up_west == lon)
    not_self_east = jnp.logical_not(self_east)
    not_self_west = jnp.logical_not(self_west)
    not_bottom = jnp.logical_not(is_bottom)

    staged = [(mask_h, mask_v), (cur_h, state_v.at[NEW]), (prev_h, state_v.at[OLD])] + [
        (ref, coef_v.at[field]) for field, ref in enumerate((es_h, em_h, ns_h, nm_h))
    ]
    loads = [pltpu.make_async_copy(a, b, in_sem.at[i]) for i, (a, b) in enumerate(staged)]

    barrier = pltpu.get_barrier_semaphore()

    def greet(to_lon, to_lat):
        pl.semaphore_signal(
            barrier, inc=1, device_id={"lon": to_lon, "lat": to_lat}, device_id_type=MESH
        )

    greet(east, lat)
    greet(west, lat)
    greet(up_main, north)

    @pl.when(not_self_east)
    def _():
        greet(up_east, north)

    @pl.when(not_self_west)
    def _():
        greet(up_west, north)

    @pl.when(not_bottom)
    def _():
        greet(lon, south)
        greet(east, south)
        greet(west, south)

    for c in loads:
        c.start()

    lane = lax.broadcasted_iota(jnp.int32, (8, LANES), 1)
    sub = lax.broadcasted_iota(jnp.int32, (8, LANES), 0)

    def roll(x, shift):
        return pltpu.roll(x, shift % LANES, 1)

    def exchange(tile):
        for bit in (1, 2, 4):
            keep = (lane & bit) == 0
            new = list(tile)
            for t in range(tiles):
                if not t & bit:
                    x, y = tile[t], tile[t + bit]
                    new[t] = jnp.where(keep, x, roll(y, bit))
                    new[t + bit] = jnp.where(keep, roll(x, -bit), y)
            tile = new
        return tile

    def lay_out(tile, target, end, r):
        rows = slice(PAD + 8 * r, PAD + 8 * r + 8)
        both = jnp.where(lane < LANES // 2, roll(tile[0], HALO), roll(tile[-1], -HALO))
        target[tiles, rows, :] = both
        end[8 * r : 8 * r + 8, :] = both
        for t, x in enumerate(exchange(tile)):
            target[t, rows, :] = x

    def block(r, t):
        return slice(8 * r, 8 * r + 8), slice(t * LANES, (t + 1) * LANES)

    for c in loads[:3]:
        c.wait()

    @pl.loop(0, 2)
    def _(lv):
        for r in range(row_tiles):
            wet = [mask_v[block(r, t)].astype(jnp.float32) for t in range(tiles)]
            for kind in (OLD, NEW):
                for tr in range(2):
                    lay_out(
                        [state_v[kind, tr, lv, *block(r, t)] * wet[t] for t in range(tiles)],
                        state.at[0, lv, kind, tr],
                        ends.at[lv, 2 * kind + tr],
                        r,
                    )

    for c in loads[3:]:
        c.wait()

    @pl.loop(0, 2)
    def _(lv):
        for field in range(4):
            for r in range(row_tiles):
                lay_out(
                    [coef_v[field, lv, *block(r, t)] * SCALES[field] for t in range(tiles)],
                    coef.at[lv, field],
                    ends.at[lv, 4 + field],
                    r,
                )

    slot_of_lane = lane // SLOT
    turn = jnp.where(is_top, -1.0, 1.0)

    @pl.loop(0, 2)
    def _(lv):
        for r in range(row_tiles):
            rows = slice(8 * r, 8 * r + 8)
            up = jnp.zeros((8, LANES), jnp.float32)
            down = jnp.zeros((8, LANES), jnp.float32)
            for s in range(8):
                here = slot_of_lane == s
                mine = ends[lv, s, rows, :]
                shift = (SLOT * s - (LANES - HALO - SLOT)) % LANES
                high = pltpu.roll(mine, shift + top, 1) if s in (4 + NS, 4 + NM) else roll(mine, shift)
                if s in (4 + ES, 4 + NS):
                    high = high * turn
                up = jnp.where(here, high, up)
                down = jnp.where(here, roll(mine, SLOT * s - HALO), down)
            pack[0, lv, rows, :] = up
            pack[1, lv, rows, :] = down

    @pl.when(is_top)
    def _():
        for h in range(2):
            turned = []
            for r in range(row_tiles):
                x = pack[0, h, 8 * r : 8 * r + 8, :]
                for bit in (1, 2, 4, 8):
                    x = jnp.where(
                        (lane & bit) == 0,
                        pltpu.roll(x, LANES - bit, 1),
                        pltpu.roll(x, bit, 1),
                    )
                for bit in (1, 2, 4):
                    x = jnp.where(
                        (sub & bit) == 0, pltpu.roll(x, 8 - bit, 0), pltpu.roll(x, bit, 0)
                    )
                turned.append(x)
            for r in range(row_tiles):
                pack[0, h, 8 * r : 8 * r + 8, :] = turned[row_tiles - 1 - r]

    @pl.when(is_bottom)
    def _():
        land[0] = jnp.zeros(land.shape[1:], jnp.float32)

    peers = 8 - jnp.where(is_bottom, 3, 0) - jnp.where(self_east, 1, 0) - jnp.where(self_west, 1, 0)
    pl.semaphore_wait(barrier, peers)

    own_rows = pl.ds(0, columns)
    last_rows, first_rows = pl.ds(columns - HALO, HALO), pl.ds(0, HALO)
    west_rows, east_rows = pl.ds(PAD - HALO, HALO), pl.ds(PAD + columns, HALO)

    def lat_copy(out, src_rows, side, dst_rows, slot, to_lon, to_lat):
        return pltpu.make_async_remote_copy(
            src_ref=pack.at[out, :, src_rows, :],
            dst_ref=land.at[side, :, dst_rows, :],
            send_sem=lat_send.at[out, slot],
            recv_sem=lat_recv.at[side, slot],
            device_id={"lon": to_lon, "lat": to_lat},
            device_id_type=MESH,
        )

    up_main_copy = lat_copy(0, own_rows, top, own, 0, up_main, north)
    up_east_copy = lat_copy(0, last_rows, top, west_rows, 1, up_east, north)
    up_west_copy = lat_copy(0, first_rows, top, east_rows, 2, up_west, north)
    down_copies = [
        lat_copy(1, own_rows, 1, own, 0, lon, south),
        lat_copy(1, last_rows, 1, west_rows, 1, east, south),
        lat_copy(1, first_rows, 1, east_rows, 2, west, south),
    ]
    self_east_copy = pltpu.make_async_copy(
        pack.at[0, :, last_rows, :], land.at[1, :, west_rows, :], self_sem.at[0]
    )
    self_west_copy = pltpu.make_async_copy(
        pack.at[0, :, first_rows, :], land.at[1, :, east_rows, :], self_sem.at[1]
    )

    up_main_copy.start()

    @pl.when(not_self_east)
    def _():
        up_east_copy.start()

    @pl.when(not_self_west)
    def _():
        up_west_copy.start()

    @pl.when(self_east)
    def _():
        self_east_copy.start()

    @pl.when(self_west)
    def _():
        self_west_copy.start()

    @pl.when(not_bottom)
    def _():
        for c in down_copies:
            c.start()

    def lon_copies(way, lv, to_lon):
        def part(source, first, target, width):
            begin = first + (columns - width if way == 0 else 0)
            dst = PAD - width if way == 0 else PAD + columns
            return source.at[..., pl.ds(begin, width), :], target.at[..., pl.ds(dst, width), :]

        main_tiles = pl.ds(0, tiles)
        new, old = state.at[0, lv, NEW, :, main_tiles], state.at[0, lv, OLD, :, main_tiles]
        east_coef = coef.at[lv, pl.ds(ES, 2), main_tiles]
        north_coef = coef.at[lv, pl.ds(NS, 2), main_tiles]
        parts = [
            part(new, PAD, new, HALO),
            part(old, PAD, old, HALO - 1),
            part(east_coef, PAD, east_coef, HALO - 1 if way == 0 else HALO - 2),
            part(north_coef, PAD, north_coef, HALO - 2),
            part(ends.at[lv, pl.ds(0, 2)], 0, state.at[0, lv, OLD, :, tiles], HALO),
            part(ends.at[lv, pl.ds(2, 2)], 0, state.at[0, lv, NEW, :, tiles], HALO),
            part(ends.at[lv, pl.ds(4, 4)], 0, coef.at[lv, :, tiles], HALO),
        ]
        return [
            pltpu.make_async_remote_copy(
                src_ref=src,
                dst_ref=dst,
                send_sem=lon_send.at[way, lv, i],
                recv_sem=lon_recv.at[way, lv, i],
                device_id={"lon": to_lon, "lat": lat},
                device_id_type=MESH,
            )
            for i, (src, dst) in enumerate(parts)
        ]

    eastward = [lon_copies(0, lv, east) for lv in range(2)]
    westward = [lon_copies(1, lv, west) for lv in range(2)]
    for lv in range(2):
        for a, b in zip(eastward[lv], westward[lv]):
            a.start()
            b.start()

    def up(x):
        return jnp.where(lane >= LANES - 8, roll(x, -9), roll(x, -8))

    def down(x):
        return jnp.where(lane < 8, roll(x, 9), roll(x, 8))

    def after(x):
        return [roll(x[0], -1)] if len(x) == 1 else x[1:] + [up(x[0])]

    def before(x):
        return [roll(x[0], 1)] if len(x) == 1 else [down(x[-1])] + x[:-1]

    def eastern(x):
        y = [pltpu.roll(a, 7, 0) for a in x]
        return [jnp.where(sub == 7, b, a) for a, b in zip(y, y[1:])] + y[-1:]

    def western(x):
        y = [pltpu.roll(a, 1, 0) for a in x]
        return y[:1] + [jnp.where(sub == 0, a, b) for a, b in zip(y, y[1:])]

    def advance(k, lv, slot, base, count, group):
        frames = [pl.ds(base + 8 * i, 8) for i in range(count)]
        old = state.at[k - 1, lv]
        for t in group:
            es = [coef[lv, ES, t, rows, :] for rows in frames]
            em = [coef[lv, EM, t, rows, :] for rows in frames]
            for tr in range(2):
                n = [old[NEW, tr, t, rows, :] for rows in frames]
                o = [old[OLD, tr, t, rows, :] for rows in frames]
                near = [a + b for a, b in zip(n, eastern(n))]
                flow = [
                    u * (8.0 * here - (a + b)) - v * (o1 - o0)
                    for u, v, here, a, b, o1, o0 in zip(
                        es, em, near, eastern(near), western(near), eastern(o), o
                    )
                ]
                for i, (a, b) in enumerate(zip(flow, western(flow))):
                    div[slot, tr, t, 8 * i : 8 * i + 8, :] = a - b
        for i, rows in enumerate(frames):
            mine = slice(8 * i, 8 * i + 8)
            for tr in range(2):
                n = [old[NEW, tr, t, rows, :] for t in group]
                o = [old[OLD, tr, t, rows, :] for t in group]
                near = [a + b for a, b in zip(n, after(n))]
                flow = [
                    coef[lv, NS, t, rows, :] * (8.0 * here - (a + b)) - coef[lv, NM, t, rows, :] * (o1 - o0)
                    for t, here, a, b, o1, o0 in zip(
                        group, near, after(near), before(near), after(o), o
                    )
                ]
                for j, (t, a, b) in enumerate(zip(group, flow, before(flow))):
                    fresh = o[j] - (div[slot, tr, t, mine, :] + (a - b))
                    held[slot, NEW, tr, t, mine, :] = fresh
                    held[slot, OLD, tr, t, mine, :] = (1.0 - 2.0 * GAMMA) * n[j] + GAMMA * (
                        o[j] + fresh
                    )

    def keep(k, lv, slot, base, windows, group):
        for kind in (NEW, OLD):
            for tr in range(2):
                for t in group:
                    for w in windows:
                        state[k, lv, kind, tr, t, pl.ds(base + w, 8), :] = held[
                            slot, kind, tr, t, w : w + 8, :
                        ]

    main, edge = list(range(tiles)), [tiles]

    def inner_place(u):
        k = jnp.where(u < 3, 1, jnp.where(u > 9, 6, (u - 3) // 2 + 2))
        j = jnp.where(u < 3, u, jnp.where(u < 9, lax.rem(u - 3, 2), 0))
        gap = jnp.where(u < 3, 8, 20 - 4 * k)
        return k, PAD + jnp.minimum(2 * k, 10) + j * gap

    @pl.loop(0, 11)
    def _(u):
        k, r0 = inner_place(u)
        for lv in range(2):
            advance(k, lv, lv, r0 - 2, 2, main)
        for lv in range(2):
            keep(k, lv, lv, r0 - 2, (2, 6), main)

    lat_in_south = [
        lat_copy(0, own_rows, 0, own, 0, lon, lat),
        lat_copy(0, last_rows, 0, west_rows, 1, lon, lat),
        lat_copy(0, first_rows, 0, east_rows, 2, lon, lat),
    ]

    @pl.when(not_bottom)
    def _():
        for c in lat_in_south:
            c.wait_recv()

    down_copies[0].wait_recv()

    @pl.when(not_self_east)
    def _():
        down_copies[1].wait_recv()

    @pl.when(not_self_west)
    def _():
        down_copies[2].wait_recv()

    @pl.when(self_east)
    def _():
        self_east_copy.wait()

    @pl.when(self_west)
    def _():
        self_west_copy.wait()

    def unpack(lv, begins):
        done = []
        for begin in begins:
            rows = pl.ds(begin, 8)
            for f in range(8):
                source = pl.ds(begin + top, 8) if f in (4 + ES, 4 + EM) else rows
                north_part = roll(land[1, lv, source, :], LANES - HALO - SLOT * f)
                south_part = roll(land[0, lv, rows, :], HALO - SLOT - SLOT * f)
                if f < 4:
                    target = state.at[0, lv, f // 2, f % 2, tiles]
                else:
                    target = coef.at[lv, f - 4, tiles]
                inside = jnp.where(lane < HALO, south_part, target[rows, :])
                done.append((target, rows, jnp.where(lane >= LANES - HALO, north_part, inside)))
        for target, rows, value in done:
            target[rows, :] = value

    @pl.loop(0, 2)
    def _(lv):
        unpack(lv, [PAD + 8 * r for r in range(row_tiles)])

    @pl.loop(1, STEPS + 1)
    def _(k):
        for lv in range(2):
            advance(k, lv, lv, PAD, row_tiles, edge)
        for lv in range(2):
            keep(k, lv, lv, PAD, range(0, columns, 8), edge)

    even = lax.rem(lon, 2) == 0

    def output_copy(kind, lv, rows, slot):
        return pltpu.make_async_copy(
            state_v.at[kind, :, lv, rows, :],
            (lag_h, lat_h)[kind].at[:, lv, rows, :],
            out_sem.at[slot, kind],
        )

    @pl.loop(0, 4)
    def _(turn_no):
        lv = lax.rem(turn_no, 2)
        do_east = even != (turn_no >= 2)

        @pl.when(do_east)
        def _():
            for c in lon_copies(1, lv, west):
                c.wait_recv()

        @pl.when(jnp.logical_not(do_east))
        def _():
            for c in lon_copies(0, lv, east):
                c.wait_recv()

        side = jnp.where(do_east, PAD + columns, PAD - HALO)
        unpack(lv, [side, side + 4])

        @pl.loop(1, STEPS + 1)
        def _(k):
            base = jnp.where(do_east, PAD + columns - 2 * k, PAD + 2 * k - UNIT) - 2
            for group in (main, edge):
                advance(k, lv, 0, base, 2, group)
            for group in (main, edge):
                keep(k, lv, 0, base, (2, 6), group)

        first = pl.multiple_of(jnp.where(do_east, columns // 2, 0), 16)
        for r in range(2):
            rows = pl.ds(pl.multiple_of(first + 8 * r, 8), 8)
            source = pl.ds(pl.multiple_of(PAD + first + 8 * r, 8), 8)
            for kind in (OLD, NEW):
                for tr in range(2):
                    tile = exchange([state[STEPS, lv, kind, tr, t, source, :] for t in main])
                    end = state[STEPS, lv, kind, tr, tiles, source, :]
                    tile[0] = jnp.where(lane < HALO, roll(end, -HALO), tile[0])
                    tile[-1] = jnp.where(lane >= LANES - HALO, roll(end, HALO), tile[-1])
                    for t in main:
                        state_v[kind, tr, lv, rows, t * LANES : (t + 1) * LANES] = tile[t]
        for kind in (OLD, NEW):
            output_copy(kind, lv, pl.ds(first, 16), turn_no).start()

    for c in sum(eastward + westward, []):
        c.wait_send()
    up_main_copy.wait_send()

    @pl.when(not_self_east)
    def _():
        up_east_copy.wait_send()

    @pl.when(not_self_west)
    def _():
        up_west_copy.wait_send()

    @pl.when(not_bottom)
    def _():
        for c in down_copies:
            c.wait_send()

    for slot in range(4):
        for kind in (OLD, NEW):
            output_copy(kind, 0, pl.ds(0, 16), slot).wait()


def solution(mesh):
    n_lon, n_lat = mesh.shape["lon"], mesh.shape["lat"]

    def shards(previous, current, east_speed, north_speed, east_mix, north_mix, sea_mask):
        columns, height = previous.shape[2:]
        tiles = height // LANES
        rows = columns + 2 * PAD
        field = jax.ShapeDtypeStruct(previous.shape, jnp.float32)
        f32 = jnp.float32
        return pl.pallas_call(
            functools.partial(kernel, (n_lon, n_lat, columns, height)),
            out_shape=(field, field),
            in_specs=[pl.BlockSpec(memory_space=pl.ANY)] * 7,
            out_specs=[pl.BlockSpec(memory_space=pl.ANY)] * 2,
            scratch_shapes=[
                pltpu.VMEM(sea_mask.shape, sea_mask.dtype),
                pltpu.VMEM((2, *previous.shape), f32),
                pltpu.VMEM((4, *east_speed.shape), f32),
                pltpu.VMEM((STEPS + 1, 2, 2, 2, tiles + 1, rows, LANES), f32),
                pltpu.VMEM((2, 4, tiles + 1, rows, LANES), f32),
                pltpu.VMEM((2, 8, columns, LANES), f32),
                pltpu.VMEM((2, 2, tiles + 1, columns, LANES), f32),
                pltpu.VMEM((2, 2, 2, tiles + 1, columns, LANES), f32),
                pltpu.VMEM((2, 2, columns, LANES), f32),
                pltpu.VMEM((2, 2, rows, LANES), f32),
                pltpu.SemaphoreType.DMA((7,)),
                pltpu.SemaphoreType.DMA((4, 2)),
                pltpu.SemaphoreType.DMA((2, 2, 7)),
                pltpu.SemaphoreType.DMA((2, 2, 7)),
                pltpu.SemaphoreType.DMA((2, 3)),
                pltpu.SemaphoreType.DMA((2, 3)),
                pltpu.SemaphoreType.DMA((2,)),
            ],
            compiler_params=pltpu.CompilerParams(
                collective_id=0, has_side_effects=True, vmem_limit_bytes=60 * 2**20
            ),
            cost_estimate=pl.CostEstimate(
                flops=30 * STEPS * previous.size, bytes_accessed=16 * previous.size, transcendentals=0
            ),
        )(previous, current, east_speed, north_speed, east_mix, north_mix, sea_mask)

    return jax.shard_map(
        shards,
        mesh=mesh,
        in_specs=(
            P(None, None, "lon", "lat"),
            P(None, None, "lon", "lat"),
            P(None, "lon", "lat"),
            P(None, "lon", "lat"),
            P(None, "lon", "lat"),
            P(None, "lon", "lat"),
            P("lon", "lat"),
        ),
        out_specs=(P(None, None, "lon", "lat"), P(None, None, "lon", "lat")),
        check_vma=False,
    )
```

time: 43 us -> 36.6 us (0.85)
  the two profiles are of different devices: /device:TPU:6 before, /device:TPU:231 now
where the time goes in v2:
time: 36.6 us; the launch traced here: 36.4 us
  Pallas kernels  33.1 us (90%)
  local copies, waits for them, and re-layouts  2.74 us (7%)
  between operations  0.65 us (2%)
    pallas_call x1, Pallas kernels, shards(): pl.pallas_call(functools.partial(kernel, (n_lon, n_lat, columns, height))...  33.1 us
    unnamed x4, local copies, waits for them, and re-layouts  2.74 us

profile of v2, /device:TPU:231, one launch (start us, length us, event | category | flops | bytes accessed | tf_op | source)
XLA Modules:
  0.0 36.4 jit_solution(610692570108047039)
XLA Ops:
  0.6 33.1 %shard_map.86 = (f32[2,2,32,1024]{3,2,1,0:T(8,128)}, f32[2,2,32,1024]{3,2,1,0:T(8,128)}) custom-call(f32[2,2,32,1024]{3,2,1,0:T(8,128)} %refs_0_.1, f32[2,2,32,1024]{3,2,1,0:T(8,128)} %refs_1_.1, f32[2,32,1024]{2,1,0:T(8,128)} %refs_2_.1, f32[2,32,1024]{2,1,0:T(8,128)} %refs_3_.1, f32[2,32,1024]{2,1,0:T(8,128)} %refs_4_.1, f32[2,32,1024]{2,1,0:T(8,128)} %refs_5_.1, ...), custom_call_target="tpu_custom_call" | custom-call | flops 23592960 | bytes 2097152 | tf_op jit(solution)/shard_map/pallas_call | solution.py:498
  33.7 0.0 copy-start
  33.7 1.9 %copy.11 = f32[2,2,32,1024]{3,2,1,0:T(8,128)} copy(f32[2,2,32,1024]{3,2,1,0:T(8,128)} %get-tuple-element.4) | data formatting | bytes 1048576
  35.6 0.0 copy-done
  35.6 0.8 %copy.12 = f32[2,2,32,1024]{3,2,1,0:T(8,128)} copy(f32[2,2,32,1024]{3,2,1,0:T(8,128)S(1)} %copy-done) | data formatting | bytes 1048576
Async XLA Ops:
  33.7 2.0 %copy-start = (f32[2,2,32,1024]{3,2,1,0:T(8,128)S(1)}, f32[2,2,32,1024]{3,2,1,0:T(8,128)}, u32[]{:S(2)}) copy-start(f32[2,2,32,1024]{3,2,1,0:T(8,128)} %get-tuple-element.5) | copy-start | bytes 1572868

commit v3 on v2

--- a/solution.py
+++ b/solution.py
@@ -18,14 +18,14 @@
 UNIT = HALO
 OLD, NEW = 0, 1
 ES, EM, NS, NM = range(4)
-SCALES = (2.0 / 12.0, 2.0, 2.0 / 12.0, 2.0)
+SCALES = (2.0 / 12.0, 2.0)
 
 
 def kernel(sizes, *refs):
     n_lon, n_lat, columns, height = sizes
     (prev_h, cur_h, es_h, ns_h, em_h, nm_h, mask_h, lag_h, lat_h) = refs[:9]
     (mask_v, state_v, coef_v, state, coef, ends, div, held, pack, land) = refs[9:19]
-    (in_sem, out_sem, lon_send, lon_recv, lat_send, lat_recv, self_sem) = refs[19:]
+    (in_sem, lon_send, lon_recv, lat_send, lat_recv, self_sem) = refs[19:]
     tiles = height // LANES
     ring = tiles + 1
     row_tiles = columns // 8
@@ -84,6 +84,9 @@
     def roll(x, shift):
         return pltpu.roll(x, shift % LANES, 1)
 
+    def permute(x, source):
+        return jnp.take_along_axis(x, source, axis=1)
+
     def exchange(tile):
         for bit in (1, 2, 4):
             keep = (lane & bit) == 0
@@ -91,8 +94,9 @@
             for t in range(tiles):
                 if not t & bit:
                     x, y = tile[t], tile[t + bit]
-                    new[t] = jnp.where(keep, x, roll(y, bit))
-                    new[t + bit] = jnp.where(keep, roll(x, -bit), y)
+                    crossing = permute(jnp.where(keep, y, x), lane ^ bit)
+                    new[t] = jnp.where(keep, x, crossing)
+                    new[t + bit] = jnp.where(keep, crossing, y)
             tile = new
         return tile
 
@@ -110,30 +114,31 @@
     for c in loads[:3]:
         c.wait()
 
-    @pl.loop(0, 2)
-    def _(lv):
+    @pl.loop(0, 4)
+    def _(i):
+        lv, kind = i // 2, lax.rem(i, 2)
         for r in range(row_tiles):
             wet = [mask_v[block(r, t)].astype(jnp.float32) for t in range(tiles)]
-            for kind in (OLD, NEW):
-                for tr in range(2):
-                    lay_out(
-                        [state_v[kind, tr, lv, *block(r, t)] * wet[t] for t in range(tiles)],
-                        state.at[0, lv, kind, tr],
-                        ends.at[lv, 2 * kind + tr],
-                        r,
-                    )
+            for tr in range(2):
+                lay_out(
+                    [state_v[kind, tr, lv, *block(r, t)] * wet[t] for t in range(tiles)],
+                    state.at[0, lv, kind, tr],
+                    ends.at[lv, 2 * kind + tr],
+                    r,
+                )
 
     for c in loads[3:]:
         c.wait()
 
-    @pl.loop(0, 2)
-    def _(lv):
-        for field in range(4):
+    @pl.loop(0, 4)
+    def _(i):
+        lv, pair = i // 2, lax.rem(i, 2)
+        for j in range(2):
             for r in range(row_tiles):
                 lay_out(
-                    [coef_v[field, lv, *block(r, t)] * SCALES[field] for t in range(tiles)],
-                    coef.at[lv, field],
-                    ends.at[lv, 4 + field],
+                    [coef_v[2 * pair + j, lv, *block(r, t)] * SCALES[j] for t in range(tiles)],
+                    coef.at[lv, 2 * pair + j],
+                    ends.at[lv, 4 + 2 * pair + j],
                     r,
                 )
 
@@ -164,12 +169,7 @@
             turned = []
             for r in range(row_tiles):
                 x = pack[0, h, 8 * r : 8 * r + 8, :]
-                for bit in (1, 2, 4, 8):
-                    x = jnp.where(
-                        (lane & bit) == 0,
-                        pltpu.roll(x, LANES - bit, 1),
-                        pltpu.roll(x, bit, 1),
-                    )
+                x = permute(x, lane ^ (SLOT - 1))
                 for bit in (1, 2, 4):
                     x = jnp.where(
                         (sub & bit) == 0, pltpu.roll(x, 8 - bit, 0), pltpu.roll(x, bit, 0)
@@ -275,17 +275,14 @@
             a.start()
             b.start()
 
-    def up(x):
-        return jnp.where(lane >= LANES - 8, roll(x, -9), roll(x, -8))
-
-    def down(x):
-        return jnp.where(lane < 8, roll(x, 9), roll(x, 8))
+    next_lane = jnp.where(lane >= LANES - 8, lane - (LANES - 9), lane + 8)
+    last_lane = jnp.where(lane < 8, lane + (LANES - 9), lane - 8)
 
     def after(x):
-        return [roll(x[0], -1)] if len(x) == 1 else x[1:] + [up(x[0])]
+        return [roll(x[0], -1)] if len(x) == 1 else x[1:] + [permute(x[0], next_lane)]
 
     def before(x):
-        return [roll(x[0], 1)] if len(x) == 1 else [down(x[-1])] + x[:-1]
+        return [roll(x[0], 1)] if len(x) == 1 else [permute(x[-1], last_lane)] + x[:-1]
 
     def eastern(x):
         y = [pltpu.roll(a, 7, 0) for a in x]
@@ -357,6 +354,49 @@
         for lv in range(2):
             keep(k, lv, lv, r0 - 2, (2, 6), main)
 
+    even = lax.rem(lon, 2) == 0
+    outs = (lag_h, lat_h)
+    wide = range((columns + 2 * HALO) // 8)
+
+    def side_in(do_east, lv):
+        @pl.when(do_east)
+        def _():
+            for c in lon_copies(1, lv, west):
+                c.wait_recv()
+
+        @pl.when(jnp.logical_not(do_east))
+        def _():
+            for c in lon_copies(0, lv, east):
+                c.wait_recv()
+
+    def side_base(do_east, k):
+        return jnp.where(do_east, PAD + columns - 2 * k, PAD + 2 * k - UNIT) - 2
+
+    def finish(do_east, lv):
+        first = pl.multiple_of(jnp.where(do_east, columns // 2, 0), 16)
+
+        @pl.loop(0, 2)
+        def _(kind_no):
+            for r in range(2):
+                rows = pl.ds(pl.multiple_of(first + 8 * r, 8), 8)
+                source = pl.ds(pl.multiple_of(PAD + first + 8 * r, 8), 8)
+                for tr in range(2):
+                    tile = exchange([state[STEPS, lv, kind_no, tr, t, source, :] for t in main])
+                    for t in main:
+                        state_v[kind_no, tr, lv, rows, t * LANES : (t + 1) * LANES] = tile[t]
+
+    @pl.loop(0, 2)
+    def _(lv):
+        side_in(even, lv)
+
+        @pl.loop(1, STEPS + 1)
+        def _(k):
+            base = side_base(even, k)
+            advance(k, lv, 0, base, 2, main)
+            keep(k, lv, 0, base, (2, 6), main)
+
+        finish(even, lv)
+
     lat_in_south = [
         lat_copy(0, own_rows, 0, own, 0, lon, lat),
         lat_copy(0, last_rows, 0, west_rows, 1, lon, lat),
@@ -405,64 +445,31 @@
 
     @pl.loop(0, 2)
     def _(lv):
-        unpack(lv, [PAD + 8 * r for r in range(row_tiles)])
-
-    @pl.loop(1, STEPS + 1)
-    def _(k):
-        for lv in range(2):
-            advance(k, lv, lv, PAD, row_tiles, edge)
-        for lv in range(2):
-            keep(k, lv, lv, PAD, range(0, columns, 8), edge)
-
-    even = lax.rem(lon, 2) == 0
-
-    def output_copy(kind, lv, rows, slot):
-        return pltpu.make_async_copy(
-            state_v.at[kind, :, lv, rows, :],
-            (lag_h, lat_h)[kind].at[:, lv, rows, :],
-            out_sem.at[slot, kind],
-        )
-
-    @pl.loop(0, 4)
-    def _(turn_no):
-        lv = lax.rem(turn_no, 2)
-        do_east = even != (turn_no >= 2)
-
-        @pl.when(do_east)
-        def _():
-            for c in lon_copies(1, lv, west):
-                c.wait_recv()
-
-        @pl.when(jnp.logical_not(do_east))
-        def _():
-            for c in lon_copies(0, lv, east):
-                c.wait_recv()
-
-        side = jnp.where(do_east, PAD + columns, PAD - HALO)
-        unpack(lv, [side, side + 4])
+        do_east = jnp.logical_not(even)
+        side_in(do_east, lv)
+        unpack(lv, [PAD - HALO + 8 * r for r in wide])
 
         @pl.loop(1, STEPS + 1)
         def _(k):
-            base = jnp.where(do_east, PAD + columns - 2 * k, PAD + 2 * k - UNIT) - 2
-            for group in (main, edge):
-                advance(k, lv, 0, base, 2, group)
-            for group in (main, edge):
-                keep(k, lv, 0, base, (2, 6), group)
-
-        first = pl.multiple_of(jnp.where(do_east, columns // 2, 0), 16)
-        for r in range(2):
-            rows = pl.ds(pl.multiple_of(first + 8 * r, 8), 8)
-            source = pl.ds(pl.multiple_of(PAD + first + 8 * r, 8), 8)
-            for kind in (OLD, NEW):
-                for tr in range(2):
-                    tile = exchange([state[STEPS, lv, kind, tr, t, source, :] for t in main])
-                    end = state[STEPS, lv, kind, tr, tiles, source, :]
-                    tile[0] = jnp.where(lane < HALO, roll(end, -HALO), tile[0])
-                    tile[-1] = jnp.where(lane >= LANES - HALO, roll(end, HALO), tile[-1])
+            base = side_base(do_east, k)
+            advance(k, lv, 0, base, 2, main)
+            advance(k, lv, 0, PAD - HALO, len(wide), edge)
+            keep(k, lv, 0, base, (2, 6), main)
+            keep(k, lv, 0, PAD - HALO, [8 * r for r in wide], edge)
+
+        finish(do_east, lv)
+        for kind in (OLD, NEW):
+            for tr in range(2):
+                for r in range(row_tiles):
+                    rows = slice(8 * r, 8 * r + 8)
+                    end = state[STEPS, lv, kind, tr, tiles, PAD + 8 * r : PAD + 8 * r + 8, :]
                     for t in main:
-                        state_v[kind, tr, lv, rows, t * LANES : (t + 1) * LANES] = tile[t]
-        for kind in (OLD, NEW):
-            output_copy(kind, lv, pl.ds(first, 16), turn_no).start()
+                        here = state_v[kind, tr, lv, rows, t * LANES : (t + 1) * LANES]
+                        if t == 0:
+                            here = jnp.where(lane < HALO, roll(end, -HALO), here)
+                        if t == tiles - 1:
+                            here = jnp.where(lane >= LANES - HALO, roll(end, HALO), here)
+                        outs[kind][tr, lv, rows, t * LANES : (t + 1) * LANES] = here
 
     for c in sum(eastward + westward, []):
         c.wait_send()
@@ -480,10 +487,6 @@
     def _():
         for c in down_copies:
             c.wait_send()
-
-    for slot in range(4):
-        for kind in (OLD, NEW):
-            output_copy(kind, 0, pl.ds(0, 16), slot).wait()
 
 
 def solution(mesh):
@@ -495,11 +498,11 @@
         rows = columns + 2 * PAD
         field = jax.ShapeDtypeStruct(previous.shape, jnp.float32)
         f32 = jnp.float32
-        return pl.pallas_call(
+        done = pl.pallas_call(
             functools.partial(kernel, (n_lon, n_lat, columns, height)),
-            out_shape=(field, field),
+            out_shape=(pltpu.VMEM(previous.shape, f32), pltpu.VMEM(previous.shape, f32)),
             in_specs=[pl.BlockSpec(memory_space=pl.ANY)] * 7,
-            out_specs=[pl.BlockSpec(memory_space=pl.ANY)] * 2,
+            out_specs=[pl.BlockSpec(memory_space=pltpu.VMEM)] * 2,
             scratch_shapes=[
                 pltpu.VMEM(sea_mask.shape, sea_mask.dtype),
                 pltpu.VMEM((2, *previous.shape), f32),
@@ -507,12 +510,11 @@
                 pltpu.VMEM((STEPS + 1, 2, 2, 2, tiles + 1, rows, LANES), f32),
                 pltpu.VMEM((2, 4, tiles + 1, rows, LANES), f32),
                 pltpu.VMEM((2, 8, columns, LANES), f32),
-                pltpu.VMEM((2, 2, tiles + 1, columns, LANES), f32),
-                pltpu.VMEM((2, 2, 2, tiles + 1, columns, LANES), f32),
+                pltpu.VMEM((2, 2, tiles + 1, rows, LANES), f32),
+                pltpu.VMEM((2, 2, 2, tiles + 1, rows, LANES), f32),
                 pltpu.VMEM((2, 2, columns, LANES), f32),
                 pltpu.VMEM((2, 2, rows, LANES), f32),
                 pltpu.SemaphoreType.DMA((7,)),
-                pltpu.SemaphoreType.DMA((4, 2)),
                 pltpu.SemaphoreType.DMA((2, 2, 7)),
                 pltpu.SemaphoreType.DMA((2, 2, 7)),
                 pltpu.SemaphoreType.DMA((2, 3)),
@@ -526,6 +528,27 @@
                 flops=30 * STEPS * previous.size, bytes_accessed=16 * previous.size, transcendentals=0
             ),
         )(previous, current, east_speed, north_speed, east_mix, north_mix, sea_mask)
+        def hand_over(a, b, x, y, sems):
+            copies = [
+                pltpu.make_async_copy(src.at[tr], dst.at[tr], sems.at[i, tr])
+                for i, (src, dst) in enumerate(((a, x), (b, y)))
+                for tr in range(2)
+            ]
+            for c in copies:
+                c.start()
+            for c in copies:
+                c.wait()
+
+        return pl.pallas_call(
+            hand_over,
+            out_shape=(field, field),
+            in_specs=[pl.BlockSpec(memory_space=pl.ANY)] * 2,
+            out_specs=[pl.BlockSpec(memory_space=pl.ANY)] * 2,
+            scratch_shapes=[pltpu.SemaphoreType.DMA((2, 2))],
+            name="hand_over",
+            compiler_params=pltpu.CompilerParams(vmem_limit_bytes=2**20),
+        )(*done)
+
 
     return jax.shard_map(
         shards,

time: 36.6 us -> 28.7 us (0.78)
  the two profiles are of different devices: /device:TPU:231 before, /device:TPU:14 now
where the time goes in v3:
time: 28.7 us; the launch traced here: 28.6 us
  Pallas kernels  28 us (98%)
  between operations  0.64 us (2%)
    pallas_call x1, Pallas kernels, shards(): pl.pallas_call(functools.partial(kernel, (n_lon, n_lat, columns, height))...  27 us
    pallas_call x1, Pallas kernels, shards(): pl.pallas_call(hand_over, out_shape=(field, field), in_specs=[pl.BlockSpe...  1 us

profile of v3, /device:TPU:14, one launch (start us, length us, event | category | flops | bytes accessed | tf_op | source)
XLA Modules:
  0.0 28.6 jit_solution(643679126204345968)
XLA Ops:
  0.6 27.0 %shard_map.86 = (f32[2,2,32,1024]{3,2,1,0:T(8,128)S(1)}, f32[2,2,32,1024]{3,2,1,0:T(8,128)S(1)}) custom-call(f32[2,2,32,1024]{3,2,1,0:T(8,128)} %refs_0_.1, f32[2,2,32,1024]{3,2,1,0:T(8,128)} %refs_1_.1, f32[2,32,1024]{2,1,0:T(8,128)} %refs_2_.1, f32[2,32,1024]{2,1,0:T(8,128)} %refs_3_.1, f32[2,32,1024]{2,1,0:T(8,128)} %refs_4_.1, f32[2,32,1024]{2,1,0:T(8,128)} %refs_5_.1, ...), custom_call_target="tpu_custom_call" | custom-call | flops 23592960 | bytes 2097152 | tf_op jit(solution)/shard_map/pallas_call | solution.py:501
  27.6 1.0 %hand_over.1 = (f32[2,2,32,1024]{3,2,1,0:T(8,128)}, f32[2,2,32,1024]{3,2,1,0:T(8,128)}) custom-call(f32[2,2,32,1024]{3,2,1,0:T(8,128)S(1)} %get-tuple-element.4.a, f32[2,2,32,1024]{3,2,1,0:T(8,128)S(1)} %get-tuple-element.5.b), custom_call_target="tpu_custom_call" | custom-call | tf_op jit(solution)/shard_map/hand_over/pallas_call | solution.py:542

commit v4 on v3

--- a/solution.py
+++ b/solution.py
@@ -16,6 +16,7 @@
 HALO = 2 * STEPS
 SLOT = 16
 UNIT = HALO
+AHEAD = 5
 OLD, NEW = 0, 1
 ES, EM, NS, NM = range(4)
 SCALES = (2.0 / 12.0, 2.0)
@@ -111,42 +112,35 @@
     def block(r, t):
         return slice(8 * r, 8 * r + 8), slice(t * LANES, (t + 1) * LANES)
 
-    for c in loads[:3]:
-        c.wait()
-
-    @pl.loop(0, 4)
-    def _(i):
-        lv, kind = i // 2, lax.rem(i, 2)
-        for r in range(row_tiles):
-            wet = [mask_v[block(r, t)].astype(jnp.float32) for t in range(tiles)]
-            for tr in range(2):
-                lay_out(
-                    [state_v[kind, tr, lv, *block(r, t)] * wet[t] for t in range(tiles)],
-                    state.at[0, lv, kind, tr],
-                    ends.at[lv, 2 * kind + tr],
-                    r,
-                )
-
-    for c in loads[3:]:
-        c.wait()
-
-    @pl.loop(0, 4)
-    def _(i):
-        lv, pair = i // 2, lax.rem(i, 2)
-        for j in range(2):
+    def lay_state(lv):
+        @pl.loop(0, 2)
+        def _(kind):
             for r in range(row_tiles):
-                lay_out(
-                    [coef_v[2 * pair + j, lv, *block(r, t)] * SCALES[j] for t in range(tiles)],
-                    coef.at[lv, 2 * pair + j],
-                    ends.at[lv, 4 + 2 * pair + j],
-                    r,
-                )
+                wet = [mask_v[block(r, t)].astype(jnp.float32) for t in range(tiles)]
+                for tr in range(2):
+                    lay_out(
+                        [state_v[kind, tr, lv, *block(r, t)] * wet[t] for t in range(tiles)],
+                        state.at[0, lv, kind, tr],
+                        ends.at[lv, 2 * kind + tr],
+                        r,
+                    )
+
+    def lay_coef(lv):
+        @pl.loop(0, 2)
+        def _(pair):
+            for j in range(2):
+                for r in range(row_tiles):
+                    lay_out(
+                        [coef_v[2 * pair + j, lv, *block(r, t)] * SCALES[j] for t in range(tiles)],
+                        coef.at[lv, 2 * pair + j],
+                        ends.at[lv, 4 + 2 * pair + j],
+                        r,
+                    )
 
     slot_of_lane = lane // SLOT
-    turn = jnp.where(is_top, -1.0, 1.0)
-
-    @pl.loop(0, 2)
-    def _(lv):
+    sign = jnp.where(is_top, -1.0, 1.0)
+
+    def pack_ends(lv):
         for r in range(row_tiles):
             rows = slice(8 * r, 8 * r + 8)
             up = jnp.zeros((8, LANES), jnp.float32)
@@ -157,85 +151,113 @@
                 shift = (SLOT * s - (LANES - HALO - SLOT)) % LANES
                 high = pltpu.roll(mine, shift + top, 1) if s in (4 + NS, 4 + NM) else roll(mine, shift)
                 if s in (4 + ES, 4 + NS):
-                    high = high * turn
+                    high = high * sign
                 up = jnp.where(here, high, up)
                 down = jnp.where(here, roll(mine, SLOT * s - HALO), down)
             pack[0, lv, rows, :] = up
             pack[1, lv, rows, :] = down
 
-    @pl.when(is_top)
-    def _():
-        for h in range(2):
+        @pl.when(is_top)
+        def _():
             turned = []
             for r in range(row_tiles):
-                x = pack[0, h, 8 * r : 8 * r + 8, :]
-                x = permute(x, lane ^ (SLOT - 1))
+                x = permute(pack[0, lv, 8 * r : 8 * r + 8, :], lane ^ (SLOT - 1))
                 for bit in (1, 2, 4):
                     x = jnp.where(
                         (sub & bit) == 0, pltpu.roll(x, 8 - bit, 0), pltpu.roll(x, bit, 0)
                     )
                 turned.append(x)
             for r in range(row_tiles):
-                pack[0, h, 8 * r : 8 * r + 8, :] = turned[row_tiles - 1 - r]
+                pack[0, lv, 8 * r : 8 * r + 8, :] = turned[row_tiles - 1 - r]
 
     @pl.when(is_bottom)
     def _():
         land[0] = jnp.zeros(land.shape[1:], jnp.float32)
 
-    peers = 8 - jnp.where(is_bottom, 3, 0) - jnp.where(self_east, 1, 0) - jnp.where(self_west, 1, 0)
-    pl.semaphore_wait(barrier, peers)
+    def wait_peers():
+        peers = 8 - jnp.where(is_bottom, 3, 0) - jnp.where(self_east, 1, 0) - jnp.where(self_west, 1, 0)
+        pl.semaphore_wait(barrier, peers)
 
     own_rows = pl.ds(0, columns)
     last_rows, first_rows = pl.ds(columns - HALO, HALO), pl.ds(0, HALO)
     west_rows, east_rows = pl.ds(PAD - HALO, HALO), pl.ds(PAD + columns, HALO)
 
-    def lat_copy(out, src_rows, side, dst_rows, slot, to_lon, to_lat):
+    def lat_copy(lv, out, src_rows, side, dst_rows, slot, to_lon, to_lat):
         return pltpu.make_async_remote_copy(
-            src_ref=pack.at[out, :, src_rows, :],
-            dst_ref=land.at[side, :, dst_rows, :],
-            send_sem=lat_send.at[out, slot],
-            recv_sem=lat_recv.at[side, slot],
+            src_ref=pack.at[out, lv, src_rows, :],
+            dst_ref=land.at[side, lv, dst_rows, :],
+            send_sem=lat_send.at[out, lv, slot],
+            recv_sem=lat_recv.at[side, lv, slot],
             device_id={"lon": to_lon, "lat": to_lat},
             device_id_type=MESH,
         )
 
-    up_main_copy = lat_copy(0, own_rows, top, own, 0, up_main, north)
-    up_east_copy = lat_copy(0, last_rows, top, west_rows, 1, up_east, north)
-    up_west_copy = lat_copy(0, first_rows, top, east_rows, 2, up_west, north)
-    down_copies = [
-        lat_copy(1, own_rows, 1, own, 0, lon, south),
-        lat_copy(1, last_rows, 1, west_rows, 1, east, south),
-        lat_copy(1, first_rows, 1, east_rows, 2, west, south),
-    ]
-    self_east_copy = pltpu.make_async_copy(
-        pack.at[0, :, last_rows, :], land.at[1, :, west_rows, :], self_sem.at[0]
-    )
-    self_west_copy = pltpu.make_async_copy(
-        pack.at[0, :, first_rows, :], land.at[1, :, east_rows, :], self_sem.at[1]
-    )
-
-    up_main_copy.start()
-
-    @pl.when(not_self_east)
-    def _():
-        up_east_copy.start()
-
-    @pl.when(not_self_west)
-    def _():
-        up_west_copy.start()
-
-    @pl.when(self_east)
-    def _():
-        self_east_copy.start()
-
-    @pl.when(self_west)
-    def _():
-        self_west_copy.start()
-
-    @pl.when(not_bottom)
-    def _():
-        for c in down_copies:
-            c.start()
+    def up_copies(lv):
+        return [
+            lat_copy(lv, 0, own_rows, top, own, 0, up_main, north),
+            lat_copy(lv, 0, last_rows, top, west_rows, 1, up_east, north),
+            lat_copy(lv, 0, first_rows, top, east_rows, 2, up_west, north),
+        ]
+
+    def down_copies(lv):
+        return [
+            lat_copy(lv, 1, own_rows, 1, own, 0, lon, south),
+            lat_copy(lv, 1, last_rows, 1, west_rows, 1, east, south),
+            lat_copy(lv, 1, first_rows, 1, east_rows, 2, west, south),
+        ]
+
+    def self_copies(lv):
+        return [
+            pltpu.make_async_copy(
+                pack.at[0, lv, last_rows, :], land.at[1, lv, west_rows, :], self_sem.at[lv, 0]
+            ),
+            pltpu.make_async_copy(
+                pack.at[0, lv, first_rows, :], land.at[1, lv, east_rows, :], self_sem.at[lv, 1]
+            ),
+        ]
+
+    def each_way(to_main, to_east, to_west, own_east, own_west, to_south):
+        to_main()
+        pl.when(not_self_east)(to_east)
+        pl.when(not_self_west)(to_west)
+        pl.when(self_east)(own_east)
+        pl.when(self_west)(own_west)
+        pl.when(not_bottom)(to_south)
+
+    def send_lat(lv):
+        ups, downs, selves = up_copies(lv), down_copies(lv), self_copies(lv)
+
+        def to_south():
+            for c in downs:
+                c.start()
+
+        each_way(ups[0].start, ups[1].start, ups[2].start, selves[0].start, selves[1].start, to_south)
+
+    def lat_in(lv):
+        norths, selves = down_copies(lv), self_copies(lv)
+
+        def from_south():
+            for slot, (src, dst) in enumerate(
+                ((own_rows, own), (last_rows, west_rows), (first_rows, east_rows))
+            ):
+                lat_copy(lv, 0, src, 0, dst, slot, lon, lat).wait_recv()
+
+        each_way(
+            norths[0].wait_recv, norths[1].wait_recv, norths[2].wait_recv,
+            selves[0].wait, selves[1].wait, from_south,
+        )
+
+    def lat_sent(lv):
+        ups, downs = up_copies(lv), down_copies(lv)
+
+        def to_south():
+            for c in downs:
+                c.wait_send()
+
+        def nothing():
+            pass
+
+        each_way(ups[0].wait_send, ups[1].wait_send, ups[2].wait_send, nothing, nothing, to_south)
 
     def lon_copies(way, lv, to_lon):
         def part(source, first, target, width):
@@ -268,10 +290,8 @@
             for i, (src, dst) in enumerate(parts)
         ]
 
-    eastward = [lon_copies(0, lv, east) for lv in range(2)]
-    westward = [lon_copies(1, lv, west) for lv in range(2)]
-    for lv in range(2):
-        for a, b in zip(eastward[lv], westward[lv]):
+    def send_lon(lv):
+        for a, b in zip(lon_copies(0, lv, east), lon_copies(1, lv, west)):
             a.start()
             b.start()
 
@@ -346,13 +366,50 @@
         gap = jnp.where(u < 3, 8, 20 - 4 * k)
         return k, PAD + jnp.minimum(2 * k, 10) + j * gap
 
-    @pl.loop(0, 11)
-    def _(u):
+    def inner_unit(u):
         k, r0 = inner_place(u)
         for lv in range(2):
             advance(k, lv, lv, r0 - 2, 2, main)
         for lv in range(2):
             keep(k, lv, lv, r0 - 2, (2, 6), main)
+
+    place = lax.rem(lon, n_lon // 2)
+    patient = jnp.logical_or(place == 0, jnp.logical_and(is_top, place < n_lon // 4))
+    ahead = jnp.where(patient, AHEAD, 0)
+    for c in loads:
+        c.wait()
+
+    @pl.loop(0, 2)
+    def _(lv):
+        lay_state(lv)
+        lay_coef(lv)
+        pack_ends(lv)
+
+        @pl.when(jnp.logical_not(patient))
+        def _():
+            @pl.when(lv == 0)
+            def _():
+                wait_peers()
+
+            send_lat(lv)
+            send_lon(lv)
+
+    @pl.when(patient)
+    def _():
+        @pl.loop(0, AHEAD)
+        def _(u):
+            inner_unit(u)
+
+        wait_peers()
+
+        @pl.loop(0, 2)
+        def _(lv):
+            send_lat(lv)
+            send_lon(lv)
+
+    @pl.loop(ahead, 11)
+    def _(u):
+        inner_unit(u)
 
     even = lax.rem(lon, 2) == 0
     outs = (lag_h, lat_h)
@@ -396,35 +453,6 @@
             keep(k, lv, 0, base, (2, 6), main)
 
         finish(even, lv)
-
-    lat_in_south = [
-        lat_copy(0, own_rows, 0, own, 0, lon, lat),
-        lat_copy(0, last_rows, 0, west_rows, 1, lon, lat),
-        lat_copy(0, first_rows, 0, east_rows, 2, lon, lat),
-    ]
-
-    @pl.when(not_bottom)
-    def _():
-        for c in lat_in_south:
-            c.wait_recv()
-
-    down_copies[0].wait_recv()
-
-    @pl.when(not_self_east)
-    def _():
-        down_copies[1].wait_recv()
-
-    @pl.when(not_self_west)
-    def _():
-        down_copies[2].wait_recv()
-
-    @pl.when(self_east)
-    def _():
-        self_east_copy.wait()
-
-    @pl.when(self_west)
-    def _():
-        self_west_copy.wait()
 
     def unpack(lv, begins):
         done = []
@@ -446,6 +474,7 @@
     @pl.loop(0, 2)
     def _(lv):
         do_east = jnp.logical_not(even)
+        lat_in(lv)
         side_in(do_east, lv)
         unpack(lv, [PAD - HALO + 8 * r for r in wide])
 
@@ -471,22 +500,11 @@
                             here = jnp.where(lane >= LANES - HALO, roll(end, HALO), here)
                         outs[kind][tr, lv, rows, t * LANES : (t + 1) * LANES] = here
 
-    for c in sum(eastward + westward, []):
-        c.wait_send()
-    up_main_copy.wait_send()
-
-    @pl.when(not_self_east)
-    def _():
-        up_east_copy.wait_send()
-
-    @pl.when(not_self_west)
-    def _():
-        up_west_copy.wait_send()
-
-    @pl.when(not_bottom)
-    def _():
-        for c in down_copies:
+    @pl.loop(0, 2)
+    def _(lv):
+        for c in lon_copies(0, lv, east) + lon_copies(1, lv, west):
             c.wait_send()
+        lat_sent(lv)
 
 
 def solution(mesh):
@@ -517,9 +535,9 @@
                 pltpu.SemaphoreType.DMA((7,)),
                 pltpu.SemaphoreType.DMA((2, 2, 7)),
                 pltpu.SemaphoreType.DMA((2, 2, 7)),
-                pltpu.SemaphoreType.DMA((2, 3)),
-                pltpu.SemaphoreType.DMA((2, 3)),
-                pltpu.SemaphoreType.DMA((2,)),
+                pltpu.SemaphoreType.DMA((2, 2, 3)),
+                pltpu.SemaphoreType.DMA((2, 2, 3)),
+                pltpu.SemaphoreType.DMA((2, 2)),
             ],
             compiler_params=pltpu.CompilerParams(
                 collective_id=0, has_side_effects=True, vmem_limit_bytes=60 * 2**20

time: 28.7 us -> 27.9 us (0.972)
  Pallas kernels: 28 us -> 27.2 us
    pallas_call x1, Pallas kernels: 27 us -> 26.2 us  [shards(): pl.pallas_call(functools.partial(kernel, (n_lon, n_lat, columns, height))...]
where the time goes in v4:
time: 27.9 us; the launch traced here: 27.8 us
  Pallas kernels  27.2 us (97%)
  between operations  0.64 us (2%)
    pallas_call x1, Pallas kernels, shards(): pl.pallas_call(functools.partial(kernel, (n_lon, n_lat, columns, height))...  26.2 us
    pallas_call x1, Pallas kernels, shards(): pl.pallas_call(hand_over, out_shape=(field, field), in_specs=[pl.BlockSpe...  1 us

profile of v4, /device:TPU:14, one launch (start us, length us, event | category | flops | bytes accessed | tf_op | source)
XLA Modules:
  0.0 27.8 jit_solution(8614325506797293109)
XLA Ops:
  0.6 26.2 %shard_map.86 = (f32[2,2,32,1024]{3,2,1,0:T(8,128)S(1)}, f32[2,2,32,1024]{3,2,1,0:T(8,128)S(1)}) custom-call(f32[2,2,32,1024]{3,2,1,0:T(8,128)} %refs_0_.1, f32[2,2,32,1024]{3,2,1,0:T(8,128)} %refs_1_.1, f32[2,32,1024]{2,1,0:T(8,128)} %refs_2_.1, f32[2,32,1024]{2,1,0:T(8,128)} %refs_3_.1, f32[2,32,1024]{2,1,0:T(8,128)} %refs_4_.1, f32[2,32,1024]{2,1,0:T(8,128)} %refs_5_.1, ...), custom_call_target="tpu_custom_call" | custom-call | flops 23592960 | bytes 2097152 | tf_op jit(solution)/shard_map/pallas_call | solution.py:519
  26.8 1.0 %hand_over.1 = (f32[2,2,32,1024]{3,2,1,0:T(8,128)}, f32[2,2,32,1024]{3,2,1,0:T(8,128)}) custom-call(f32[2,2,32,1024]{3,2,1,0:T(8,128)S(1)} %get-tuple-element.4.a, f32[2,2,32,1024]{3,2,1,0:T(8,128)S(1)} %get-tuple-element.5.b), custom_call_target="tpu_custom_call" | custom-call | tf_op jit(solution)/shard_map/hand_over/pallas_call | solution.py:560

commit v5 on v4

--- a/solution.py
+++ b/solution.py
@@ -16,7 +16,7 @@
 HALO = 2 * STEPS
 SLOT = 16
 UNIT = HALO
-AHEAD = 5
+FIRST = 5
 OLD, NEW = 0, 1
 ES, EM, NS, NM = range(4)
 SCALES = (2.0 / 12.0, 2.0)
@@ -260,20 +260,23 @@
         each_way(ups[0].wait_send, ups[1].wait_send, ups[2].wait_send, nothing, nothing, to_south)
 
     def lon_copies(way, lv, to_lon):
-        def part(source, first, target, width):
-            begin = first + (columns - width if way == 0 else 0)
-            dst = PAD - width if way == 0 else PAD + columns
+        main_tiles = pl.ds(0, tiles)
+
+        def part(source, first, target, width, skip=0):
+            begin = first + (columns - skip - width if way == 0 else skip)
+            dst = PAD - skip - width if way == 0 else PAD + columns + skip
             return source.at[..., pl.ds(begin, width), :], target.at[..., pl.ds(dst, width), :]
 
-        main_tiles = pl.ds(0, tiles)
-        new, old = state.at[0, lv, NEW, :, main_tiles], state.at[0, lv, OLD, :, main_tiles]
-        east_coef = coef.at[lv, pl.ds(ES, 2), main_tiles]
-        north_coef = coef.at[lv, pl.ds(NS, 2), main_tiles]
+        def main_part(ref, width, skip=0):
+            return part(ref, PAD, ref, width, skip)
+
         parts = [
-            part(new, PAD, new, HALO),
-            part(old, PAD, old, HALO - 1),
-            part(east_coef, PAD, east_coef, HALO - 1 if way == 0 else HALO - 2),
-            part(north_coef, PAD, north_coef, HALO - 2),
+            main_part(state.at[k, lv, kind, :, main_tiles], width, 2 * k)
+            for k in range(3)
+            for kind, width in ((NEW, 4), (OLD, 3))
+        ] + [
+            main_part(coef.at[lv, pl.ds(ES, 2), main_tiles], 7 if way == 0 else 6),
+            main_part(coef.at[lv, pl.ds(NS, 2), main_tiles], 6),
             part(ends.at[lv, pl.ds(0, 2)], 0, state.at[0, lv, OLD, :, tiles], HALO),
             part(ends.at[lv, pl.ds(2, 2)], 0, state.at[0, lv, NEW, :, tiles], HALO),
             part(ends.at[lv, pl.ds(4, 4)], 0, coef.at[lv, :, tiles], HALO),
@@ -290,10 +293,13 @@
             for i, (src, dst) in enumerate(parts)
         ]
 
-    def send_lon(lv):
-        for a, b in zip(lon_copies(0, lv, east), lon_copies(1, lv, west)):
-            a.start()
-            b.start()
+    def send_lon(lv, parts):
+        a, b = lon_copies(0, lv, east), lon_copies(1, lv, west)
+        for i in parts:
+            a[i].start()
+            b[i].start()
+
+    AT_ONCE, STEPPED = (0, 1, 6, 7, 8, 9, 10), (2, 3, 4, 5)
 
     next_lane = jnp.where(lane >= LANES - 8, lane - (LANES - 9), lane + 8)
     last_lane = jnp.where(lane < 8, lane + (LANES - 9), lane - 8)
@@ -366,16 +372,15 @@
         gap = jnp.where(u < 3, 8, 20 - 4 * k)
         return k, PAD + jnp.minimum(2 * k, 10) + j * gap
 
-    def inner_unit(u):
+    def inner_unit(u, levels):
         k, r0 = inner_place(u)
-        for lv in range(2):
-            advance(k, lv, lv, r0 - 2, 2, main)
-        for lv in range(2):
-            keep(k, lv, lv, r0 - 2, (2, 6), main)
+        for slot, lv in enumerate(levels):
+            advance(k, lv, slot, r0 - 2, 2, main)
+        for slot, lv in enumerate(levels):
+            keep(k, lv, slot, r0 - 2, (2, 6), main)
 
     place = lax.rem(lon, n_lon // 2)
     patient = jnp.logical_or(place == 0, jnp.logical_and(is_top, place < n_lon // 4))
-    ahead = jnp.where(patient, AHEAD, 0)
     for c in loads:
         c.wait()
 
@@ -392,24 +397,28 @@
                 wait_peers()
 
             send_lat(lv)
-            send_lon(lv)
+            send_lon(lv, AT_ONCE)
+
+        @pl.loop(0, FIRST)
+        def _(u):
+            inner_unit(u, [lv])
+
+        @pl.when(jnp.logical_not(patient))
+        def _():
+            send_lon(lv, STEPPED)
 
     @pl.when(patient)
     def _():
-        @pl.loop(0, AHEAD)
-        def _(u):
-            inner_unit(u)
-
         wait_peers()
 
         @pl.loop(0, 2)
         def _(lv):
             send_lat(lv)
-            send_lon(lv)
-
-    @pl.loop(ahead, 11)
+            send_lon(lv, AT_ONCE + STEPPED)
+
+    @pl.loop(FIRST, 11)
     def _(u):
-        inner_unit(u)
+        inner_unit(u, range(2))
 
     even = lax.rem(lon, 2) == 0
     outs = (lag_h, lat_h)
@@ -420,14 +429,19 @@
         def _():
             for c in lon_copies(1, lv, west):
                 c.wait_recv()
+            for c in lon_copies(0, lv, east):
+                c.wait_send()
 
         @pl.when(jnp.logical_not(do_east))
         def _():
             for c in lon_copies(0, lv, east):
                 c.wait_recv()
+            for c in lon_copies(1, lv, west):
+                c.wait_send()
 
     def side_base(do_east, k):
-        return jnp.where(do_east, PAD + columns - 2 * k, PAD + 2 * k - UNIT) - 2
+        west_base = jnp.maximum(2 * k - UNIT, -2 * k)
+        return jnp.where(do_east, PAD + columns - UNIT - west_base, PAD + west_base) - 2
 
     def finish(do_east, lv):
         first = pl.multiple_of(jnp.where(do_east, columns // 2, 0), 16)
@@ -502,8 +516,6 @@
 
     @pl.loop(0, 2)
     def _(lv):
-        for c in lon_copies(0, lv, east) + lon_copies(1, lv, west):
-            c.wait_send()
         lat_sent(lv)
 
 
@@ -533,8 +545,8 @@
                 pltpu.VMEM((2, 2, columns, LANES), f32),
                 pltpu.VMEM((2, 2, rows, LANES), f32),
                 pltpu.SemaphoreType.DMA((7,)),
-                pltpu.SemaphoreType.DMA((2, 2, 7)),
-                pltpu.SemaphoreType.DMA((2, 2, 7)),
+                pltpu.SemaphoreType.DMA((2, 2, 11)),
+                pltpu.SemaphoreType.DMA((2, 2, 11)),
                 pltpu.SemaphoreType.DMA((2, 2, 3)),
                 pltpu.SemaphoreType.DMA((2, 2, 3)),
                 pltpu.SemaphoreType.DMA((2, 2)),

time: 27.9 us -> 26.4 us (0.946)
  Pallas kernels: 27.2 us -> 25.7 us
    pallas_call x1, Pallas kernels: 26.2 us -> 24.7 us  [shards(): pl.pallas_call(functools.partial(kernel, (n_lon, n_lat, columns, height))...]
where the time goes in v5:
time: 26.4 us; the launch traced here: 26.3 us
  Pallas kernels  25.7 us (97%)
  between operations  0.64 us (2%)
    pallas_call x1, Pallas kernels, shards(): pl.pallas_call(functools.partial(kernel, (n_lon, n_lat, columns, height))...  24.7 us
    pallas_call x1, Pallas kernels, shards(): pl.pallas_call(hand_over, out_shape=(field, field), in_specs=[pl.BlockSpe...  1 us

profile of v5, /device:TPU:14, one launch (start us, length us, event | category | flops | bytes accessed | tf_op | source)
XLA Modules:
  0.0 26.3 jit_solution(9023565103804311137)
XLA Ops:
  0.6 24.7 %shard_map.86 = (f32[2,2,32,1024]{3,2,1,0:T(8,128)S(1)}, f32[2,2,32,1024]{3,2,1,0:T(8,128)S(1)}) custom-call(f32[2,2,32,1024]{3,2,1,0:T(8,128)} %refs_0_.1, f32[2,2,32,1024]{3,2,1,0:T(8,128)} %refs_1_.1, f32[2,32,1024]{2,1,0:T(8,128)} %refs_2_.1, f32[2,32,1024]{2,1,0:T(8,128)} %refs_3_.1, f32[2,32,1024]{2,1,0:T(8,128)} %refs_4_.1, f32[2,32,1024]{2,1,0:T(8,128)} %refs_5_.1, ...), custom_call_target="tpu_custom_call" | custom-call | flops 23592960 | bytes 2097152 | tf_op jit(solution)/shard_map/pallas_call | solution.py:531
  25.3 1.0 %hand_over.1 = (f32[2,2,32,1024]{3,2,1,0:T(8,128)}, f32[2,2,32,1024]{3,2,1,0:T(8,128)}) custom-call(f32[2,2,32,1024]{3,2,1,0:T(8,128)S(1)} %get-tuple-element.4.a, f32[2,2,32,1024]{3,2,1,0:T(8,128)S(1)} %get-tuple-element.5.b), custom_call_target="tpu_custom_call" | custom-call | tf_op jit(solution)/shard_map/hand_over/pallas_call | solution.py:572

commit v6 on v5

--- a/solution.py
+++ b/solution.py
@@ -299,7 +299,7 @@
             a[i].start()
             b[i].start()
 
-    AT_ONCE, STEPPED = (0, 1, 6, 7, 8, 9, 10), (2, 3, 4, 5)
+    AT_ONCE, STEPPED = (0, 1, 8, 9, 6, 7, 10), (2, 3, 4, 5)
 
     next_lane = jnp.where(lane >= LANES - 8, lane - (LANES - 9), lane + 8)
     last_lane = jnp.where(lane < 8, lane + (LANES - 9), lane - 8)
@@ -381,14 +381,12 @@
 
     place = lax.rem(lon, n_lon // 2)
     patient = jnp.logical_or(place == 0, jnp.logical_and(is_top, place < n_lon // 4))
-    for c in loads:
+    for c in loads[:3]:
         c.wait()
 
     @pl.loop(0, 2)
     def _(lv):
         lay_state(lv)
-        lay_coef(lv)
-        pack_ends(lv)
 
         @pl.when(jnp.logical_not(patient))
         def _():
@@ -396,8 +394,24 @@
             def _():
                 wait_peers()
 
+            send_lon(lv, AT_ONCE[:4])
+
+        @pl.when(lv == 0)
+        def _():
+            for c in loads[3:]:
+                c.wait()
+
+        lay_coef(lv)
+
+        @pl.when(jnp.logical_not(patient))
+        def _():
+            send_lon(lv, AT_ONCE[4:])
+
+        pack_ends(lv)
+
+        @pl.when(jnp.logical_not(patient))
+        def _():
             send_lat(lv)
-            send_lon(lv, AT_ONCE)
 
         @pl.loop(0, FIRST)
         def _(u):
@@ -446,15 +460,14 @@
     def finish(do_east, lv):
         first = pl.multiple_of(jnp.where(do_east, columns // 2, 0), 16)
 
-        @pl.loop(0, 2)
-        def _(kind_no):
+        for kind in (OLD, NEW):
             for r in range(2):
                 rows = pl.ds(pl.multiple_of(first + 8 * r, 8), 8)
                 source = pl.ds(pl.multiple_of(PAD + first + 8 * r, 8), 8)
                 for tr in range(2):
-                    tile = exchange([state[STEPS, lv, kind_no, tr, t, source, :] for t in main])
+                    tile = exchange([state[STEPS, lv, kind, tr, t, source, :] for t in main])
                     for t in main:
-                        state_v[kind_no, tr, lv, rows, t * LANES : (t + 1) * LANES] = tile[t]
+                        state_v[kind, tr, lv, rows, t * LANES : (t + 1) * LANES] = tile[t]
 
     @pl.loop(0, 2)
     def _(lv):

time: 26.4 us -> 25.6 us (0.970)
  the two profiles are of different devices: /device:TPU:14 before, /device:TPU:3 now
where the time goes in v6:
time: 25.6 us; the launch traced here: 25.5 us
  Pallas kernels  24.8 us (97%)
  between operations  0.64 us (2%)
    pallas_call x1, Pallas kernels, shards(): pl.pallas_call(functools.partial(kernel, (n_lon, n_lat, columns, height))...  23.8 us
    pallas_call x1, Pallas kernels, shards(): pl.pallas_call(hand_over, out_shape=(field, field), in_specs=[pl.BlockSpe...  1 us

profile of v6, /device:TPU:3, one launch (start us, length us, event | category | flops | bytes accessed | tf_op | source)
XLA Modules:
  0.0 25.5 jit_solution(2214821629814511008)
XLA Ops:
  0.6 23.8 %shard_map.86 = (f32[2,2,32,1024]{3,2,1,0:T(8,128)S(1)}, f32[2,2,32,1024]{3,2,1,0:T(8,128)S(1)}) custom-call(f32[2,2,32,1024]{3,2,1,0:T(8,128)} %refs_0_.1, f32[2,2,32,1024]{3,2,1,0:T(8,128)} %refs_1_.1, f32[2,32,1024]{2,1,0:T(8,128)} %refs_2_.1, f32[2,32,1024]{2,1,0:T(8,128)} %refs_3_.1, f32[2,32,1024]{2,1,0:T(8,128)} %refs_4_.1, f32[2,32,1024]{2,1,0:T(8,128)} %refs_5_.1, ...), custom_call_target="tpu_custom_call" | custom-call | flops 23592960 | bytes 2097152 | tf_op jit(solution)/shard_map/pallas_call | solution.py:544
  24.5 1.0 %hand_over.1 = (f32[2,2,32,1024]{3,2,1,0:T(8,128)}, f32[2,2,32,1024]{3,2,1,0:T(8,128)}) custom-call(f32[2,2,32,1024]{3,2,1,0:T(8,128)S(1)} %get-tuple-element.4.a, f32[2,2,32,1024]{3,2,1,0:T(8,128)S(1)} %get-tuple-element.5.b), custom_call_target="tpu_custom_call" | custom-call | tf_op jit(solution)/shard_map/hand_over/pallas_call | solution.py:585

commit v7 on v6

--- a/solution.py
+++ b/solution.py
@@ -467,7 +467,7 @@
                 for tr in range(2):
                     tile = exchange([state[STEPS, lv, kind, tr, t, source, :] for t in main])
                     for t in main:
-                        state_v[kind, tr, lv, rows, t * LANES : (t + 1) * LANES] = tile[t]
+                        outs[kind][tr, lv, rows, t * LANES : (t + 1) * LANES] = tile[t]
 
     @pl.loop(0, 2)
     def _(lv):
@@ -519,8 +519,8 @@
                 for r in range(row_tiles):
                     rows = slice(8 * r, 8 * r + 8)
                     end = state[STEPS, lv, kind, tr, tiles, PAD + 8 * r : PAD + 8 * r + 8, :]
-                    for t in main:
-                        here = state_v[kind, tr, lv, rows, t * LANES : (t + 1) * LANES]
+                    for t in (0, tiles - 1):
+                        here = outs[kind][tr, lv, rows, t * LANES : (t + 1) * LANES]
                         if t == 0:
                             here = jnp.where(lane < HALO, roll(end, -HALO), here)
                         if t == tiles - 1:

time: 25.6 us -> 25.5 us (level)
  no operation moved by 1% of the time
where the time goes in v7:
time: 25.5 us; the launch traced here: 25.4 us
  Pallas kernels  24.8 us (97%)
  between operations  0.64 us (3%)
    pallas_call x1, Pallas kernels, shards(): pl.pallas_call(functools.partial(kernel, (n_lon, n_lat, columns, height))...  23.8 us
    pallas_call x1, Pallas kernels, shards(): pl.pallas_call(hand_over, out_shape=(field, field), in_specs=[pl.BlockSpe...  1 us

profile of v7, /device:TPU:3, one launch (start us, length us, event | category | flops | bytes accessed | tf_op | source)
XLA Modules:
  0.0 25.4 jit_solution(1307483145184070893)
XLA Ops:
  0.6 23.8 %shard_map.86 = (f32[2,2,32,1024]{3,2,1,0:T(8,128)S(1)}, f32[2,2,32,1024]{3,2,1,0:T(8,128)S(1)}) custom-call(f32[2,2,32,1024]{3,2,1,0:T(8,128)} %refs_0_.1, f32[2,2,32,1024]{3,2,1,0:T(8,128)} %refs_1_.1, f32[2,32,1024]{2,1,0:T(8,128)} %refs_2_.1, f32[2,32,1024]{2,1,0:T(8,128)} %refs_3_.1, f32[2,32,1024]{2,1,0:T(8,128)} %refs_4_.1, f32[2,32,1024]{2,1,0:T(8,128)} %refs_5_.1, ...), custom_call_target="tpu_custom_call" | custom-call | flops 23592960 | bytes 2097152 | tf_op jit(solution)/shard_map/pallas_call | solution.py:544
  24.4 1.0 %hand_over.1 = (f32[2,2,32,1024]{3,2,1,0:T(8,128)}, f32[2,2,32,1024]{3,2,1,0:T(8,128)}) custom-call(f32[2,2,32,1024]{3,2,1,0:T(8,128)S(1)} %get-tuple-element.4.a, f32[2,2,32,1024]{3,2,1,0:T(8,128)S(1)} %get-tuple-element.5.b), custom_call_target="tpu_custom_call" | custom-call | tf_op jit(solution)/shard_map/hand_over/pallas_call | solution.py:585
